TPU v7x, 128 devices: a whole 4x4x4 slice. The times are simulated.
128 devices in a mesh: tm: 8 (over x, core), sy: 4 (over z), sx: 4 (over y).
Axes of the slice: x: 4, y: 4, z: 4, core: 2. Of those that a mesh axis runs over, the one named last changes fastest.
Arguments:
- latent_init: float32 [64, 96, 320], P('sy', 'sx'), may hold values from -80 to 80
- step_noise: bfloat16 [32, 64, 96, 320], P('tm', 'sy', 'sx'), may hold values from -6 to 6
- coef_state: float32 [32], P('tm'), may hold values from -0.06 to -0.01
- coef_drift: float32 [32], P('tm'), may hold values from -0.1 to 0.1
- coef_noise: float32 [32], P('tm'), may hold values from 0.05 to 0.2
- step_index: int32 [32], P('tm'), may hold values from 0 to 999
- time_table: float32 [1000, 320], replicated, may hold values from -1.5 to 1.5
- norm_gain: float32 [320], replicated, may hold values from 0.25 to 1.75
- conv_weight: bfloat16 [3, 3, 320, 320], replicated, may hold values from -0.109375 to 0.109375
- reward_grad: float32 [64, 96, 320], P('sy', 'sx'), may hold values from -0.18 to 0.18
Outputs:
- trajectory: float32 [32, 64, 96, 320], P('tm', 'sy', 'sx')
- grad_weight: float32 [3, 3, 320, 320], P(None, None, None, 'tm')
All inputs are finite; a program needn't handle non-finite values.
Results may differ from a plain program's by a relative error of at most 0.0009.
The roundings to bfloat16 on the way count: a program that leaves them out, or rounds other values in their place, can miss the bound.
Values may be sent and summed in bfloat16 or wider, within the bound.
A program may use at most 128 MiB of HBM per device.

v0:
```python
import jax
import jax.numpy as jnp
from jax import lax
from jax.sharding import PartitionSpec as P

GROUPS = 32
ITERS = 2


EPSILON = 1e-05


def prefix(value, axis, join, neutral, backward):
    count, mine = (lax.axis_size(axis), lax.axis_index(axis))
    pieces = lax.all_gather(value, axis)
    if backward:
        pieces = pieces[::-1]
        mine = count - 1 - mine
    subtotal = jnp.full_like(value, 0) + jnp.asarray(neutral, value.dtype)

    def step(position, subtotal):
        longer = join(subtotal, pieces[position])
        return jnp.where(position < mine, longer, subtotal)

    return lax.fori_loop(0, count - 1, step, subtotal)


def with_halo(block, sides, width):
    for axis, dim in sides:
        count = lax.axis_size(axis)
        forward = [(i, i + 1) for i in range(count - 1)]
        backward = [(target, source) for source, target in forward]
        low = lax.ppermute(
            lax.slice_in_dim(block, block.shape[dim] - width, None, axis=dim), axis, forward
        )
        high = lax.ppermute(lax.slice_in_dim(block, 0, width, axis=dim), axis, backward)
        block = jnp.concatenate([low, block, high], axis=dim)
    return block


def add_terms(earlier, later):
    return earlier + later


def lower_total(block_total, reverse):
    return prefix(block_total, "tm", add_terms, jnp.zeros_like(block_total), reverse)


def group_count(tile_rows, tile_cols, channels):
    return tile_rows * lax.axis_size("sy") * tile_cols * lax.axis_size("sx") * (channels // GROUPS)


def group_stats(grouped, cell_count):
    totals = lax.psum(jnp.sum(grouped, axis=(1, 3)), ("sy", "sx"))
    center = totals / cell_count
    shifted = grouped - center[:, None, :, None]
    spread = lax.psum(jnp.sum(shifted * shifted, axis=(1, 3)), ("sy", "sx")) / cell_count
    return (shifted, spread)


def prepare(states, modulate):
    steps_here, tile_rows, tile_cols, channels = states.shape
    grouped = states.reshape(steps_here, tile_rows * tile_cols, GROUPS, channels // GROUPS)
    shifted, spread = group_stats(grouped, group_count(tile_rows, tile_cols, channels))
    inv_std = 1.0 / jnp.sqrt(spread + EPSILON)
    normal_field = (shifted * inv_std[:, None, :, None]).reshape(states.shape)
    pre_act = normal_field * modulate[:, None, None, :]
    activation = jax.nn.silu(pre_act).astype(jnp.bfloat16)
    act_pad = with_halo(activation, (("sy", 1), ("sx", 2)), 1)
    return (normal_field, inv_std, pre_act, act_pad)


def convolve(act_pad, conv_weight, tile_rows, tile_cols):
    result = jnp.zeros(
        act_pad.shape[:1] + (tile_rows, tile_cols, conv_weight.shape[3]), jnp.float32
    )
    for row_off in range(3):
        for col_off in range(3):
            window = act_pad[:, row_off : row_off + tile_rows, col_off : col_off + tile_cols, :]
            result = result + jnp.einsum(
                "bhwc,cd->bhwd",
                window,
                conv_weight[row_off, col_off],
                preferred_element_type=jnp.float32,
            )
    return result


def backprop(upstream, act_cache, modulate, conv_weight, need_state):
    normal_field, inv_std, pre_act, act_pad = act_cache
    steps_here, tile_rows, tile_cols, channels = upstream.shape
    up_half = upstream.astype(jnp.bfloat16)
    weight_rows = []
    for row_off in range(3):
        weight_cols = []
        for col_off in range(3):
            window = act_pad[:, row_off : row_off + tile_rows, col_off : col_off + tile_cols, :]
            weight_cols.append(
                jnp.einsum("bhwc,bhwd->cd", window, up_half, preferred_element_type=jnp.float32)
            )
        weight_rows.append(jnp.stack(weight_cols))
    grad_piece = jnp.stack(weight_rows)
    if not need_state:
        return (upstream, grad_piece)
    up_pad = with_halo(up_half, (("sy", 1), ("sx", 2)), 1)
    d_act = jnp.zeros(upstream.shape, jnp.float32)
    for row_off in range(3):
        for col_off in range(3):
            window = up_pad[
                :, 2 - row_off : 2 - row_off + tile_rows, 2 - col_off : 2 - col_off + tile_cols, :
            ]
            d_act = d_act + jnp.einsum(
                "bhwd,cd->bhwc",
                window,
                conv_weight[row_off, col_off],
                preferred_element_type=jnp.float32,
            )
    sig_value = jax.nn.sigmoid(pre_act)
    d_norm = d_act * sig_value * (1.0 + pre_act * (1.0 - sig_value)) * modulate[:, None, None, :]
    group_shape = (steps_here, tile_rows * tile_cols, GROUPS, channels // GROUPS)
    grouped_d = d_norm.reshape(group_shape)
    grouped_n = normal_field.reshape(group_shape)
    cell_count = group_count(tile_rows, tile_cols, channels)
    plain_sum, cross_sum = lax.psum(
        (jnp.sum(grouped_d, axis=(1, 3)), jnp.sum(grouped_d * grouped_n, axis=(1, 3))), ("sy", "sx")
    )
    plain_mean = plain_sum / cell_count
    cross_mean = cross_sum / cell_count
    d_group = (
        grouped_d - plain_mean[:, None, :, None] - grouped_n * cross_mean[:, None, :, None]
    ) * inv_std[:, None, :, None]
    return (upstream + d_group.reshape(upstream.shape), grad_piece)


def shards(
    latent_init,
    step_noise,
    coef_state,
    coef_drift,
    coef_noise,
    step_index,
    time_table,
    norm_gain,
    conv_weight,
    reward_grad,
):
    tile_rows, tile_cols = (step_noise.shape[1], step_noise.shape[2])
    table_ids = jnp.arange(time_table.shape[0], dtype=jnp.int32)
    one_hot = (step_index[:, None] == table_ids[None, :]).astype(jnp.float32)
    embedded = jnp.dot(one_hot, time_table, precision=lax.Precision.HIGHEST)
    modulate = norm_gain[None, :] * (1.0 + embedded)
    state_c = coef_state[:, None, None, None]
    drift_c = coef_drift[:, None, None, None]
    noise_c = coef_noise[:, None, None, None]
    states = jnp.broadcast_to(latent_init[None], step_noise.shape)
    saved_states = []
    caches = []
    trajectory = states
    for sweep_index in range(ITERS):
        saved_states.append(states)
        act_cache = prepare(states, modulate)
        caches.append(act_cache)
        drift_term = states + convolve(act_cache[3], conv_weight, tile_rows, tile_cols)
        increment = (
            state_c * states + drift_c * drift_term + noise_c * step_noise.astype(jnp.float32)
        )
        running = jnp.cumsum(increment, axis=0)
        offset = lower_total(running[-1], False)
        trajectory = latent_init[None] + (offset[None] + running)
        if sweep_index + 1 < ITERS:
            before = jnp.concatenate([jnp.zeros_like(running[:1]), running[:-1]], axis=0)
            states = latent_init[None] + (offset[None] + before)
    adjoint = jnp.broadcast_to(reward_grad[None], step_noise.shape)
    grad_total = jnp.zeros(conv_weight.shape, jnp.float32)
    for sweep_index in range(ITERS - 1, -1, -1):
        act_cache = prepare(saved_states[sweep_index], modulate)
        upstream = drift_c * adjoint
        d_state, grad_piece = backprop(upstream, act_cache, modulate, conv_weight, sweep_index > 0)
        grad_total = grad_total + grad_piece
        if sweep_index > 0:
            through = state_c * adjoint + d_state
            suffix = jnp.cumsum(through[::-1], axis=0)[::-1]
            higher = lower_total(suffix[0], True)
            after = jnp.concatenate([suffix[1:], jnp.zeros_like(suffix[:1])], axis=0)
            adjoint = higher[None] + after
    share = lax.psum_scatter(grad_total, "tm", scatter_dimension=3, tiled=True)
    grad_weight = lax.psum(share, ("sy", "sx"))
    return (trajectory, grad_weight)


def solution(mesh):
    placed = (
        P("sy", "sx", None),
        P("tm", "sy", "sx", None),
        P("tm"),
        P("tm"),
        P("tm"),
        P("tm"),
        P(),
        P(),
        P(),
        P("sy", "sx", None),
    )
    return jax.shard_map(
        shards,
        mesh=mesh,
        in_specs=placed,
        out_specs=(P("tm", "sy", "sx", None), P(None, None, None, "tm")),
        check_vma=False,
    )
```

profile of v0, /device:TPU:0, one launch (start us, length us, event | category | flops | bytes accessed | tf_op | source)
XLA Modules:
  0.0 634.7 jit_solution(18137577999258617183)
XLA Ops:
  8.7 42.0 %psum.46 = f32[4,32]{1,0:T(4,128)S(1)} all-reduce(f32[4,32]{1,0:T(4,128)S(1)} %reduce_sum.117), channel_id=1, replica_groups=mesh['tm'=8,'sy'=4,'sx'=4] {'sy','sx'}, use_global_device_ids=true, to_apply=%region_2.0 | all-reduce | flops 128 | bytes 1024 | tf_op jit(solution)/shard_map/psum | solution.py:54
  52.5 35.5 %psum.49 = f32[4,32]{1,0:T(4,128)S(1)} all-reduce(f32[4,32]{1,0:T(4,128)S(1)} %reduce_sum.120), channel_id=1, replica_groups=mesh['tm'=8,'sy'=4,'sx'=4] {'sy','sx'}, use_global_device_ids=true, to_apply=%region_5.6 | all-reduce | flops 128 | bytes 1024 | tf_op jit(solution)/shard_map/psum | solution.py:57
  98.3 3.9 collective-permute-start.2
  123.3 6.3 fusion.33
  142.3 4.8 collective-permute-start.11
  166.7 8.7 %while.42 = (s32[]{:T(128)}, f32[16,24,320]{2,1,0:T(8,128)S(1)}, s32[]{:T(128)}, f32[8,16,24,320]{3,2,1,0:T(8,128)}, s32[]{:T(128)}, /*index=5*/s32[]{:T(128)}) while((s32[]{:T(128)}, f32[16,24,320]{2,1,0:T(8,128)S(1)}, s32[]{:T(128)}, f32[8,16,24,320]{3,2,1,0:T(8,128)}, s32[]{:T(128)}, /*index=5*/s32[]{:T(128)}) %tuple.106), condition=%wide.region_8.9_spmd.clone, body=%wide.region_7.8_spmd.clone.sunk | while | flops 368644 | bytes 1474653 | solution.py:25
  177.4 39.4 %psum.50 = f32[4,32]{1,0:T(4,128)S(1)} all-reduce(f32[4,32]{1,0:T(4,128)S(1)} %reduce_sum.123), channel_id=1, replica_groups=mesh['tm'=8,'sy'=4,'sx'=4] {'sy','sx'}, use_global_device_ids=true, to_apply=%region_11.12 | all-reduce | flops 128 | bytes 1024 | tf_op jit(solution)/shard_map/psum | solution.py:54
  222.4 36.1 %psum.51 = f32[4,32]{1,0:T(4,128)} all-reduce(f32[4,32]{1,0:T(4,128)} %reduce_sum.126), channel_id=1, replica_groups=mesh['tm'=8,'sy'=4,'sx'=4] {'sy','sx'}, use_global_device_ids=true, to_apply=%region_14.15 | all-reduce | flops 128 | bytes 1024 | tf_op jit(solution)/shard_map/psum | solution.py:57
  261.5 11.5 %fusion.219 = (f32[4,320]{1,0:T(4,128)}, f32[4,320]{1,0:T(4,128)}, f32[4,16,24,320]{3,2,1,0:T(8,128)}) fusion(f32[4,320]{1,0:T(4,128)} %mul.201, f32[4,320]{1,0:T(4,128)S(1)} %sub.66, f32[3,16,24,320]{3,2,1,0:T(8,128)S(1)} %slice.280, f32[16,24,320]{2,1,0:T(8,128)S(1)} %get-tuple-element.239, f32[16,24,320]{2,1,0:T(8,128)S(1)} %copy-done.2, ...), kind=kOutput, calls=%fused_computation.276 | convolution fusion | flops 326858240 | bytes 24750080 | tf_op jit(solution)/shard_map/bhwd,cd->bhwc/dot_general | solution.py:112
  278.9 38.7 %all-reduce.3 = (f32[4,32]{1,0:T(4,128)}, f32[4,32]{1,0:T(4,128)}) all-reduce(f32[4,32]{1,0:T(4,128)} %reduce_sum.132, f32[4,32]{1,0:T(4,128)} %reduce_sum.129), channel_id=1, replica_groups=mesh['tm'=8,'sy'=4,'sx'=4] {'sy','sx'}, use_global_device_ids=true, to_apply=%region_23.24 | all-reduce | flops 256 | bytes 2048 | tf_op jit(solution)/shard_map/psum | solution.py:124
  324.0 5.2 fusion.18
  344.9 3.5 fusion.162
  357.1 3.8 fusion.146
  381.7 4.9 rev.8
  386.6 8.7 %while.44 = (s32[]{:T(128)}, f32[16,24,320]{2,1,0:T(8,128)S(1)}, s32[]{:T(128)}, f32[8,16,24,320]{3,2,1,0:T(8,128)}, s32[]{:T(128)}, /*index=5*/s32[]{:T(128)}) while((s32[]{:T(128)}, f32[16,24,320]{2,1,0:T(8,128)S(1)}, s32[]{:T(128)}, f32[8,16,24,320]{3,2,1,0:T(8,128)}, s32[]{:T(128)}, /*index=5*/s32[]{:T(128)}) %tuple.112), condition=%wide.region_26.27_spmd.clone, body=%wide.region_25.26_spmd.clone.sunk | while | flops 368644 | bytes 1474653 | solution.py:25
  410.3 8.4 %copy.14 = f32[3,3,320,320]{2,1,0,3:T(4,128)} copy(f32[3,3,320,320]{3,2,1,0:T(8,128)} %maximum_add_fusion) | data formatting | bytes 7372800 | tf_op jit(solution)/shard_map/add | solution.py:179
  419.0 3.9 fusion.113
  422.9 3.6 fusion.116
  430.0 3.5 fusion.122
  437.0 8.6 %fusion.19 = f32[4,16,24,320]{3,2,1,0:T(8,128)S(1)} fusion(f32[4,16,24,320]{3,2,1,0:T(8,128)} %fusion.110, f32[4,16,24,320]{3,2,1,0:T(8,128)} %fusion.145, f32[4,16,24,320]{3,2,1,0:T(8,128)} %fusion.113, f32[4,16,24,320]{3,2,1,0:T(8,128)} %fusion.116, f32[4,16,24,320]{3,2,1,0:T(8,128)} %fusion.162, f32[4,16,24,320]{3,2,1,0:T(8,128)} %fusion.119, ...), kind=kOutput, calls=%fused_computation.31 | output fusion | flops 9830400 | bytes 23101488 | tf_op jit(solution)/shard_map/jit(cumsum)/reduce_window_sum | solution.py:167
  449.3 51.1 %all-reduce.9.cloned.1.call-done = f32[3,3,320,320]{2,1,0,3:T(4,128)} async-done(((f32[3,3,320,320]{2,1,0,3:T(4,128)}), f32[3,3,320,320]{2,1,0,3:T(4,128)}) %all-reduce.9.cloned.1.call-update) | async-done | bytes 3686416
  502.5 33.7 %all-gather.6.cloned.1.call-done = f32[8,16,24,320]{3,2,1,0:T(8,128)} async-done(((f32[1,16,24,320]{3,2,1,0:T(8,128)}), f32[8,16,24,320]{3,2,1,0:T(8,128)}) %all-gather.6.cloned.1.call-update) | async-done | bytes 3932176 | tf_op jit(solution)/shard_map/all_gather | solution.py:15
  536.2 8.7 %while.43 = (s32[]{:T(128)}, f32[16,24,320]{2,1,0:T(8,128)S(1)}, s32[]{:T(128)}, f32[8,16,24,320]{3,2,1,0:T(8,128)}, s32[]{:T(128)}, /*index=5*/s32[]{:T(128)}) while((s32[]{:T(128)}, f32[16,24,320]{2,1,0:T(8,128)S(1)}, s32[]{:T(128)}, f32[8,16,24,320]{3,2,1,0:T(8,128)}, s32[]{:T(128)}, /*index=5*/s32[]{:T(128)}) %tuple.109), condition=%wide.region_17.18_spmd.clone, body=%wide.region_16.17_spmd.clone.sunk | while | flops 368644 | bytes 1474653 | solution.py:25
  548.2 77.7 %all-reduce.7.cloned.1.call-done = f32[3,3,320,40]{2,1,0,3:T(4,128)} async-done(((f32[3,3,320,40]{2,1,0,3:T(4,128)}), f32[3,3,320,40]{2,1,0,3:T(4,128)}) %all-reduce.7.cloned.1.call-update) | async-done | bytes 460816 | tf_op jit(solution)/shard_map/psum | solution.py:187
  (263 shorter events, 192.4 us)
Async XLA Ops:
  7.2 81.0 %copy-start = (f32[1000,320]{0,1:T(8,128)S(1)}, f32[1000,320]{0,1:T(8,128)}, u32[]{:S(2)}) copy-start(f32[1000,320]{0,1:T(8,128)} %param.22) | copy-start | bytes 3840004
  7.2 82.6 %copy-start.2 = (f32[16,24,320]{2,1,0:T(8,128)S(1)}, f32[16,24,320]{2,1,0:T(8,128)}, u32[]{:S(2)}) copy-start(f32[16,24,320]{2,1,0:T(8,128)} %param.16) | copy-start | bytes 1474564
  7.2 159.5 %all-gather.4.cloned.1.call-start = ((), (), s32[]{:S(2)}) async-start(), calls=%async_computation | async-start | bytes 5308416 | tf_op jit(solution)/shard_map/all_gather | solution.py:15
  51.0 44.8 %copy-start.39 = (f32[4,320]{1,0:T(4,128)}, f32[4,320]{1,0:T(4,128)S(1)}, u32[]{:S(2)}) copy-start(f32[4,320]{1,0:T(4,128)S(1)} %sub.62) | copy-start | bytes 15364
  90.5 18.4 %copy-start.5 = (bf16[4,16,24,320]{3,2,1,0:T(8,128)(2,1)}, bf16[4,16,24,320]{3,2,1,0:T(8,128)(2,1)S(1)}, u32[]{:S(2)}) copy-start(bf16[4,16,24,320]{3,2,1,0:T(8,128)(2,1)S(1)} %fusion.17) | copy-start | bytes 2949124
  90.5 5.2 collective-permute-start
  91.8 6.2 collective-permute-start.1
  95.8 13.1 %copy-start.32 = (bf16[4,1,24,320]{3,2,1,0:T(8,128)(2,1)}, bf16[4,1,24,320]{3,2,1,0:T(8,128)(2,1)S(1)}, u32[]{:S(2)}) copy-start(bf16[4,1,24,320]{3,2,1,0:T(8,128)(2,1)S(1)} %collective-permute-done) | copy-start | bytes 184324
  98.3 7.5 %collective-permute-start.2 = (bf16[4,18,1,320]{3,2,1,0:T(2,128)(2,1)S(1)}, bf16[4,18,1,320]{3,2,1,0:T(2,128)(2,1)S(1)}, u32[]{:S(2)}, u32[]{:S(2)}) collective-permute-start(bf16[4,18,1,320]{3,2,1,0:T(2,128)(2,1)S(1)} %get-tuple-element.333), channel_id=1, source_target_pairs={{0,1},{1,2},{2,3},{4,5},{5,6},{6,7},{8,9},{9,10},{10,11},{12,13},{... | collective-permute-start | bytes 138248 | tf_op jit(solution)/shard_map/ppermute | solution.py:33
  102.2 6.6 %collective-permute-start.3 = (bf16[4,18,1,320]{3,2,1,0:T(2,128)(2,1)S(1)}, bf16[4,18,1,320]{3,2,1,0:T(2,128)(2,1)S(1)}, u32[]{:S(2)}, u32[]{:S(2)}) collective-permute-start(bf16[4,18,1,320]{3,2,1,0:T(2,128)(2,1)S(1)} %get-tuple-element.334), channel_id=1, source_target_pairs={{1,0},{2,1},{3,2},{5,4},{6,5},{7,6},{9,8},{10,9},{11,10},{13,12},{... | collective-permute-start | bytes 138248 | tf_op jit(solution)/shard_map/ppermute | solution.py:36
  131.9 249.8 %all-gather.8.cloned.1.call-start = ((), (), s32[]{:S(2)}) async-start(), calls=%async_computation.2 | async-start | bytes 5308416 | tf_op jit(solution)/shard_map/all_gather | solution.py:15
  132.3 18.1 %copy-start.7 = (bf16[4,16,24,320]{3,2,1,0:T(8,128)(2,1)}, bf16[4,16,24,320]{3,2,1,0:T(8,128)(2,1)S(1)}, u32[]{:S(2)}) copy-start(bf16[4,16,24,320]{3,2,1,0:T(8,128)(2,1)S(1)} %multiply_convert_fusion) | copy-start | bytes 2949124
  132.3 6.9 %collective-permute-start.8 = (bf16[4,1,24,320]{3,2,1,0:T(8,128)(2,1)S(1)}, bf16[4,1,24,320]{3,2,1,0:T(8,128)(2,1)S(1)}, u32[]{:S(2)}, u32[]{:S(2)}) collective-permute-start(bf16[4,1,24,320]{3,2,1,0:T(8,128)(2,1)S(1)} %get-tuple-element.336), channel_id=1, source_target_pairs={{0,4},{4,8},{8,12},{1,5},{5,9},{9,13},{2,6},{6,10},{10,14},{3,7},{... | collective-permute-start | bytes 184328 | tf_op jit(solution)/shard_map/ppermute | solution.py:33
  134.6 6.2 collective-permute-start.9
  141.0 11.9 %collective-permute-start.10 = (bf16[4,18,1,320]{3,2,1,0:T(2,128)(2,1)S(1)}, bf16[4,18,1,320]{3,2,1,0:T(2,128)(2,1)S(1)}, u32[]{:S(2)}, u32[]{:S(2)}) collective-permute-start(bf16[4,18,1,320]{3,2,1,0:T(2,128)(2,1)S(1)} %get-tuple-element.326), channel_id=1, source_target_pairs={{1,0},{2,1},{3,2},{5,4},{6,5},{7,6},{9,8},{10,9},{11,10},{13,12},{... | collective-permute-start | bytes 138248 | tf_op jit(solution)/shard_map/ppermute | solution.py:36
  142.3 10.6 %collective-permute-start.11 = (bf16[4,18,1,320]{3,2,1,0:T(2,128)(2,1)S(1)}, bf16[4,18,1,320]{3,2,1,0:T(2,128)(2,1)S(1)}, u32[]{:S(2)}, u32[]{:S(2)}) collective-permute-start(bf16[4,18,1,320]{3,2,1,0:T(2,128)(2,1)S(1)} %get-tuple-element.325), channel_id=1, source_target_pairs={{0,1},{1,2},{2,3},{4,5},{5,6},{6,7},{8,9},{9,10},{10,11},{12,13},{... | collective-permute-start | bytes 138248 | tf_op jit(solution)/shard_map/ppermute | solution.py:33
  336.6 163.8 %all-reduce.9.cloned.1.call-start = ((), (), s32[]{:S(2)}) async-start(), calls=%async_computation.4 | async-start | bytes 11796480
  338.2 14.3 %collective-permute-start.4 = (bf16[4,1,24,320]{3,2,1,0:T(8,128)(2,1)}, bf16[4,1,24,320]{3,2,1,0:T(8,128)(2,1)}, u32[]{:S(2)}, u32[]{:S(2)}) collective-permute-start(bf16[4,1,24,320]{3,2,1,0:T(8,128)(2,1)} %get-tuple-element.337), channel_id=1, source_target_pairs={{0,4},{4,8},{8,12},{1,5},{5,9},{9,13},{2,6},{6,10},{10,14},{3,7},{... | collective-permute-start | bytes 184328 | tf_op jit(solution)/shard_map/ppermute | solution.py:33
  340.2 12.4 %collective-permute-start.5 = (bf16[4,1,24,320]{3,2,1,0:T(8,128)(2,1)}, bf16[4,1,24,320]{3,2,1,0:T(8,128)(2,1)}, u32[]{:S(2)}, u32[]{:S(2)}) collective-permute-start(bf16[4,1,24,320]{3,2,1,0:T(8,128)(2,1)} %get-tuple-element.338), channel_id=1, source_target_pairs={{4,0},{8,4},{12,8},{5,1},{9,5},{13,9},{6,2},{10,6},{14,10},{7,3},{... | collective-permute-start | bytes 184328 | tf_op jit(solution)/shard_map/ppermute | solution.py:36
  354.0 13.5 %collective-permute-start.6 = (bf16[4,18,1,320]{3,2,1,0:T(2,128)(2,1)S(1)}, bf16[4,18,1,320]{3,2,1,0:T(2,128)(2,1)S(1)}, u32[]{:S(2)}, u32[]{:S(2)}) collective-permute-start(bf16[4,18,1,320]{3,2,1,0:T(2,128)(2,1)S(1)} %get-tuple-element.329), channel_id=1, source_target_pairs={{0,1},{1,2},{2,3},{4,5},{5,6},{6,7},{8,9},{9,10},{10,11},{12,13},{... | collective-permute-start | bytes 138248 | tf_op jit(solution)/shard_map/ppermute | solution.py:33
  355.8 11.8 %collective-permute-start.7 = (bf16[4,18,1,320]{3,2,1,0:T(2,128)(2,1)S(1)}, bf16[4,18,1,320]{3,2,1,0:T(2,128)(2,1)S(1)}, u32[]{:S(2)}, u32[]{:S(2)}) collective-permute-start(bf16[4,18,1,320]{3,2,1,0:T(2,128)(2,1)S(1)} %get-tuple-element.330), channel_id=1, source_target_pairs={{1,0},{2,1},{3,2},{5,4},{6,5},{7,6},{9,8},{10,9},{11,10},{13,12},{... | collective-permute-start | bytes 138248 | tf_op jit(solution)/shard_map/ppermute | solution.py:36
  418.8 117.4 %all-gather.6.cloned.1.call-start = ((), (), s32[]{:S(2)}) async-start(), calls=%async_computation.1 | async-start | bytes 5308416 | tf_op jit(solution)/shard_map/all_gather | solution.py:15
  447.9 178.1 %all-reduce.7.cloned.1.call-start = ((), (), s32[]{:S(2)}) async-start(), calls=%async_computation.3 | async-start | bytes 1474560 | tf_op jit(solution)/shard_map/psum | solution.py:187
  544.9 83.0 %copy-start.1 = (f32[1000,320]{0,1:T(8,128)S(1)}, f32[1000,320]{0,1:T(8,128)}, u32[]{:S(2)}) copy-start(f32[1000,320]{0,1:T(8,128)} %param.22) | copy-start | bytes 3840004
  (43 other events, 196.4 us)
Sparse Core Ops, SparseCore 0:
  132.0 33.4 all-gather.3
  336.7 29.2 all-gather.7
  418.9 81.4 all-reduce.8
  502.0 34.1 all-gather.5
  539.7 86.2 all-reduce.6
where the time goes:
time: 641 us; the launch traced here: 635 us
  blocking collectives  192 us (30%)
  waiting for transfers between devices  170 us (27%)
  matrix products  101 us (16%)
  other arithmetic  78.3 us (12%)
  local copies, waits for them, and re-layouts  53.7 us (8%)
  starting transfers between devices  24.5 us (4%)
  between operations  15.5 us (2%)
    psum x2, blocking collectives, group_stats(): totals = lax.psum(jnp.sum(grouped, axis=(1, 3)), ('sy', 'sx'))  81.4 us
    psum x1, waiting for transfers between devices, shards(): grad_weight = lax.psum(share, ('sy', 'sx'))  77.7 us
    psum x2, blocking collectives, group_stats(): lax.psum(jnp.sum(shifted * shifted, axis=(1, 3)), ('sy', 'sx')) / cell_count  71.6 us
    unnamed x6, waiting for transfers between devices  51.2 us
    dot_general x18, matrix products, convolve(): jnp.einsum('bhwc,cd->bhwd', window, conv_weight[row_off, col_off], prefer...  49.7 us
    psum x1, blocking collectives, backprop(): lax.psum((jnp.sum(grouped_d, axis=(1, 3)), jnp.sum(grouped_d * grouped_n,...  38.7 us
    all_gather x3, waiting for transfers between devices, prefix(): pieces = lax.all_gather(value, axis)  33.7 us
    dot_general x9, matrix products, backprop(): jnp.einsum('bhwd,cd->bhwc', window, conv_weight[row_off, col_off], prefer...  31.9 us
  transfers between devices with their start and end apart: 17, of which 6 were waited for; matrix products, arithmetic and copies ran while one was open for 17% of the time, Pallas kernels for 0%

commit v1 on v0

v1 whole, which is shorter than its diff:
```python
import functools
import itertools

import jax
import jax.numpy as jnp
from jax import lax
from jax.experimental import pallas as pl
from jax.experimental.pallas import tpu as pltpu
from jax.sharding import PartitionSpec as P

MESH = pl.DeviceIdType.MESH
VM = pl.BlockSpec(memory_space=pltpu.VMEM)
SM = pl.BlockSpec(memory_space=pltpu.SMEM)
F32 = jnp.float32
BF16 = jnp.bfloat16
HI = lax.Precision.HIGHEST
EPSILON = 1e-05
GSIZE = 10
T = 4
H = 16
W = 24
C = 320
PW = 32
HP = H + 2
AW = 1024
VLIM = 60 << 20


def rcopy(src, dst, ssem, rsem, dev):
    return pltpu.make_async_remote_copy(
        src_ref=src, dst_ref=dst, send_sem=ssem, recv_sem=rsem, device_id=dev, device_id_type=MESH
    )


def greet(devs):
    sem = pltpu.get_barrier_semaphore()
    for dev in devs:
        pl.semaphore_signal(sem, inc=1, device_id=dev, device_id_type=MESH)
    pl.semaphore_wait(sem, len(devs))


class Where:
    def __init__(self, dims):
        self.nt, self.ny, self.nx = dims
        self.tm = lax.axis_index("tm")
        self.y = lax.axis_index("sy")
        self.x = lax.axis_index("sx")
        self.nd = self.ny * self.nx
        self.me = self.y * self.nx + self.x

    def dev(self, tm, y, x):
        return (tm, y, x)

    def tile(self, d):
        q = lax.rem(self.me + d, self.nd)
        return q, self.dev(self.tm, lax.div(q, self.nx), lax.rem(q, self.nx))

    def shift(self, dy, dx):
        return self.dev(
            self.tm,
            lax.rem(self.y + dy + self.ny, self.ny),
            lax.rem(self.x + dx + self.nx, self.nx),
        )

    def tiles(self):
        return [self.tile(d)[1] for d in range(1, self.nd)]

    def line(self):
        c = lax.rem(self.tm, 2)
        return [
            self.dev(self.tm + 1 - 2 * c, self.y, self.x),
            self.dev(lax.rem(self.tm + 2, self.nt), self.y, self.x),
            self.dev(lax.rem(self.tm + self.nt - 2, self.nt), self.y, self.x),
        ]


def gather_start(w, buf, ssem, rsem):
    out = []
    for d in range(1, w.nd):
        _, dev = w.tile(d)
        cp = rcopy(buf.at[w.me], buf.at[w.me], ssem.at[d], rsem.at[w.me], dev)
        cp.start()
        out.append(cp)
    return out


def gather_wait(w, buf, ssem, rsem, sent):
    for cp in sent:
        cp.wait_send()
    for d in range(1, w.nd):
        q, dev = w.tile(d)
        rcopy(buf.at[q], buf.at[q], ssem.at[d], rsem.at[q], dev).wait_recv()


def group_matrix():
    row = lax.broadcasted_iota(jnp.int32, (C, C), 0)
    col = lax.broadcasted_iota(jnp.int32, (C, C), 1)
    same = ((row * 6554) >> 16) == ((col * 6554) >> 16)
    return same.astype(F32)


def moments(buf, w):
    gm = group_matrix()
    n = float(H * W)
    both = buf[...]
    mean = jnp.sum(both[:, 0:T], axis=0) * (1.0 / w.nd)
    center = jnp.dot(mean, gm, precision=HI, preferred_element_type=F32) * (1.0 / GSIZE)
    off = both[:, 0:T] - center[None]
    dev = jnp.sum(both[:, T:] + n * off * off, axis=0)
    total = jnp.dot(dev, gm, precision=HI, preferred_element_type=F32)
    spread = total * (1.0 / (n * w.nd * GSIZE))
    return center, 1.0 / jnp.sqrt(spread + EPSILON)


SIDES = ((0, -1), (0, 1), (-1, 0), (1, 0), (-1, -1), (-1, 1), (1, -1), (1, 1))


def halo_pack(p, n, col_s, cor_s):
    for f in range(n):
        col_s[0, f] = p[f, 1 : 1 + H, 0, :]
        col_s[1, f] = p[f, 1 : 1 + H, W - 1, :]
        for j, (dy, dx) in enumerate(SIDES[4:]):
            row = 1 if dy < 0 else H
            lane = 0 if dx < 0 else W - 1
            cor_s[j, f : f + 1, :] = p[f, row, lane : lane + 1, :]


def halo_copies(w, p, col_s, col_r, cor_s, cor_r, ssem, rsem):
    out = []
    for j, (dy, dx) in enumerate(SIDES):
        dev = w.shift(dy, dx)
        if j < 2:
            src, dst = col_s.at[j], col_r.at[j]
        elif j < 4:
            row, land = (1, HP - 1) if dy < 0 else (H, 0)
            src, dst = p.at[:, row, 0:W, :], p.at[:, land, 0:W, :]
        else:
            src, dst = cor_s.at[j - 4], cor_r.at[j - 4]
        out.append(rcopy(src, dst, ssem.at[j], rsem.at[j], dev))
    return out


def halo_unpack(p, n, col_r, cor_r):
    for f in range(n):
        p[f, 1 : 1 + H, W, :] = col_r[0, f]
        p[f, 1 : 1 + H, PW - 1, :] = col_r[1, f]
        for j, (dy, dx) in enumerate(SIDES[4:]):
            row = HP - 1 if dy < 0 else 0
            lane = W if dx < 0 else PW - 1
            p[f, row, lane : lane + 1, :] = cor_r[j, f : f + 1, :]


def halo_scratch(n):
    return [
        pltpu.VMEM((2, n, H, C), F32),
        pltpu.VMEM((2, n, H, C), F32),
        pltpu.VMEM((4, 8, C), F32),
        pltpu.VMEM((4, 8, C), F32),
        pltpu.SemaphoreType.DMA((8,)),
        pltpu.SemaphoreType.DMA((8,)),
    ]


def gather_scratch(nd):
    return [
        pltpu.VMEM((nd, 8, C), F32),
        pltpu.SemaphoreType.DMA((nd,)),
        pltpu.SemaphoreType.DMA((nd,)),
    ]


def tile_moments(read, n):
    cells = 1.0 / (H * W)
    means, devs = [], []
    for f in range(n):

        def add(i, acc, f=f):
            return acc + read(f, i)

        total = lax.fori_loop(0, H, add, jnp.zeros((W, C), F32), unroll=4)
        mean = jnp.sum(total, axis=0, keepdims=True) * cells

        def add2(i, acc, f=f, mean=mean):
            v = read(f, i) - mean
            return acc + v * v

        total = lax.fori_loop(0, H, add2, jnp.zeros((W, C), F32), unroll=4)
        means.append(mean)
        devs.append(jnp.sum(total, axis=0, keepdims=True))
    return means, devs


def k_open(dims, lat, rg, p, st, *scratch):
    w = Where(dims)
    hal, gat = scratch[:6], scratch[6:]
    col_s, col_r, cor_s, cor_r, hs, hr = hal
    buf, gs, gr = gat

    def fill(i, _):
        for f, ref in ((0, lat), (1, rg)):
            p[f, i + 1, 0:W, :] = ref[i]
            p[f, i + 1, W:PW, :] = jnp.zeros((PW - W, C), F32)
        return 0

    lax.fori_loop(0, H, fill, 0)
    for f in range(2):
        for row in (0, HP - 1):
            p[f, row] = jnp.zeros((PW, C), F32)
    cor_s[...] = jnp.zeros_like(cor_s)
    halo_pack(p, 2, col_s, cor_s)
    greet(w.tiles())
    copies = halo_copies(w, p, col_s, col_r, cor_s, cor_r, hs, hr)
    for cp in copies:
        cp.start()
    means, devs = tile_moments(lambda f, i: lat[i], 1)
    buf[w.me] = jnp.concatenate(means * T + devs * T, axis=0)
    sent = gather_start(w, buf, gs, gr)
    gather_wait(w, buf, gs, gr, sent)
    center, inv = moments(buf, w)
    st[0:T] = center
    st[T:] = inv
    for cp in copies:
        cp.wait()
    halo_unpack(p, 2, col_r, cor_r)


def edge_mask(w, i):
    col = lax.broadcasted_iota(jnp.int32, (PW, 1), 0)
    rows = jnp.logical_and(
        jnp.logical_or(i > 0, w.y > 0), jnp.logical_or(i < HP - 1, w.y < w.ny - 1)
    )
    left = jnp.where(w.x > 0, 1, 0)
    right = jnp.where(w.x < w.nx - 1, 1, 0)
    inside = jnp.where(col == PW - 1, left, jnp.where(col == W, right, 1))
    return inside * jnp.where(rows, 1, 0) > 0


def pack_row(ab, k, i, v):
    shifts = [pltpu.roll(v, 1, 0)[0:W], v[0:W], pltpu.roll(v, PW - 1, 0)[0:W]]
    for s in range(3):
        ab[k, i, :, 256 * s : 256 * s + 256] = shifts[s][:, 0:256].astype(BF16)
    tail = jnp.concatenate(
        [u[:, 256:C] for u in shifts] + [jnp.zeros((W, 64), F32)], axis=1
    )
    ab[k, i, :, 768:AW] = tail.astype(BF16)


def window(ab, k, r):
    return ab[k, r : r + H].reshape(H * W, AW)


def conv(ab, k, wt):
    acc = jnp.dot(window(ab, k, 0), wt[0], preferred_element_type=F32)
    acc += jnp.dot(window(ab, k, 1), wt[1], preferred_element_type=F32)
    acc += jnp.dot(window(ab, k, 2), wt[2], preferred_element_type=F32)
    return acc.reshape(H, W, C)


def build_act(w, p, st, mod, ab, k, f):
    center = st[pl.ds(k, 1), :]
    inv = st[pl.ds(T + k, 1), :]
    m = mod[pl.ds(k, 1), :]

    def row(i, _):
        pre = (p[f, i] - center) * inv * m
        act = pre / (1.0 + jnp.exp(-pre))
        act = jnp.where(edge_mask(w, i), act, 0.0)
        pack_row(ab, k, i, act)
        return 0

    lax.fori_loop(0, HP, row, 0, unroll=2)


def k_first(dims, coef, p, st, mod, wr, wd, noise, run, ab, dact, abu):
    w = Where(dims)

    def step(k, _):
        cs, cd, cn = coef[0, k], coef[1, k], coef[2, k]
        build_act(w, p, st, mod, ab, k, 0)
        out = conv(ab, k, wr)
        lat = p[0, 1 : 1 + H, 0:W, :]
        inc = cs * lat + cd * (lat + out) + cn * noise[k].astype(F32)
        prev = run[jnp.maximum(k - 1, 0)]
        run[k] = jnp.where(k > 0, prev, 0.0) + inc

        def row(i, _):
            up = jnp.where(edge_mask(w, i), cd * p[1, i], 0.0)
            pack_row(abu, k, i, up)
            return 0

        lax.fori_loop(0, HP, row, 0, unroll=2)
        dact[k] = conv(abu, k, wd)
        return 0

    lax.fori_loop(0, T, step, 0)


def k_second(dims, coef, p, st, mod, wr, noise, dact, run, ab, dn, cs_out):
    w = Where(dims)

    def step(k, _):
        cs, cd, cn = coef[0, k], coef[1, k], coef[2, k]
        build_act(w, p, st, mod, ab, k, k)
        out = conv(ab, k, wr)
        v = p[k, 1 : 1 + H, 0:W, :]
        inc = cs * v + cd * (v + out) + cn * noise[k].astype(F32)
        prev = run[jnp.maximum(k - 1, 0)]
        run[k] = jnp.where(k > 0, prev, 0.0) + inc
        center = st[pl.ds(k, 1), :]
        inv = st[pl.ds(T + k, 1), :]
        m = mod[pl.ds(k, 1), :]

        def row(i, acc):
            plain, cross = acc
            norm = (p[k, i + 1, 0:W, :] - center) * inv
            pre = norm * m
            sig = 1.0 / (1.0 + jnp.exp(-pre))
            d = dact[k, i] * sig * (1.0 + pre * (1.0 - sig)) * m
            dn[k, i] = d
            return plain + d, cross + d * norm

        zero = jnp.zeros((W, C), F32)
        plain, cross = lax.fori_loop(0, H, row, (zero, zero), unroll=2)
        cs_out[pl.ds(k, 1), :] = jnp.sum(plain, axis=0, keepdims=True)
        cs_out[pl.ds(T + k, 1), :] = jnp.sum(cross, axis=0, keepdims=True)
        return 0

    lax.fori_loop(0, T, step, 0)


def k_weight(dims, coef, rg, adj, ab1, ab2, g, upt):
    for k in range(T):
        cd = coef[1, k]
        up1 = (cd * adj[k]).reshape(H * W, C).astype(BF16)
        up2 = (cd * rg[...]).reshape(H * W, C).astype(BF16)
        upt[:, pl.ds(k * H * W, H * W)] = up1.T
        upt[:, pl.ds((T + k) * H * W, H * W)] = up2.T
    nt = dims[0]
    for r in range(3):
        for j in range(AW // 256):
            rhs = [
                ab[k, r : r + H, :, 256 * j : 256 * j + 256].reshape(H * W, 256)
                for ab in (ab1, ab2)
                for k in range(T)
            ]
            out = jnp.dot(
                upt[...], jnp.concatenate(rhs, axis=0), preferred_element_type=F32
            )
            for half in range(2):
                chunk = r * 8 + j * 2 + half
                part = out[:, 128 * half : 128 * half + 128]
                g[:, 5 * chunk : 5 * chunk + 5] = part.reshape(nt, 5, 8, 128)
    g[:, 120:128] = jnp.zeros((nt, 8, 8, 128), F32)


CHUNKS = 4


def chain_scratch():
    half = (H // 2, W, C)
    return [
        pltpu.VMEM(half, F32),
        pltpu.VMEM(half, F32),
        pltpu.VMEM(half, F32),
        pltpu.VMEM(half, F32),
        pltpu.VMEM((H, W, C), F32),
        pltpu.SemaphoreType.DMA((1 + 2 * CHUNKS,)),
        pltpu.SemaphoreType.DMA((1 + 2 * CHUNKS,)),
    ]


def chain_start(w, total, scr, rev):
    prx, inc, outc, offp, off, ss, rs = scr
    hh = H // 2
    c = lax.rem(w.tm, 2)
    partner = w.line()[0]
    cp = rcopy(total.at[pl.ds(hh * (1 - c), hh)], prx, ss.at[0], rs.at[0], partner)
    cp.start()


def chain_steps(w, total, scr, rev):
    prx, inc, outc, offp, off, ss, rs = scr
    hh = H // 2
    per = hh // CHUNKS
    c = lax.rem(w.tm, 2)
    x = lax.div(w.tm, 2)
    chips = w.nt // 2
    partner, nxt, prv = w.line()
    if rev:
        nxt, prv = prv, nxt
        x = chips - 1 - x
    second = (c == 0) if rev else (c == 1)
    cp0 = rcopy(total.at[pl.ds(hh * (1 - c), hh)], prx, ss.at[0], rs.at[0], partner)
    cp0.wait_recv()

    @pl.when(x == 0)
    def _():
        inc[...] = jnp.zeros_like(inc)

    def fwd(j):
        part = pl.ds(j * per, per)
        return rcopy(outc.at[part], inc.at[part], ss.at[1 + j], rs.at[1 + j], nxt)

    def give(j):
        part = pl.ds(j * per, per)
        return rcopy(
            offp.at[part],
            off.at[pl.ds(hh * c + j * per, per)],
            ss.at[1 + CHUNKS + j],
            rs.at[1 + CHUNKS + j],
            partner,
        )

    for j in range(CHUNKS):
        part = pl.ds(j * per, per)
        own = pl.ds(hh * c + j * per, per)

        @pl.when(x > 0)
        def _():
            fwd(j).wait_recv()

        got = inc[part]
        mine = total[own]
        other = prx[part]

        @pl.when(x < chips - 1)
        def _():
            outc[part] = got + (mine + other)
            fwd(j).start()

        off[own] = got + jnp.where(second, other, 0.0)
        offp[part] = got + jnp.where(second, 0.0, mine)
        give(j).start()
        yield
    cp0.wait_send()
    for j in range(CHUNKS):
        give(j).wait_send()
        rcopy(
            offp.at[pl.ds(j * per, per)],
            off.at[pl.ds(hh * (1 - c) + j * per, per)],
            ss.at[1 + CHUNKS + j],
            rs.at[1 + CHUNKS + j],
            partner,
        ).wait_recv()

        @pl.when(x < chips - 1)
        def _():
            fwd(j).wait_send()


def k_states(dims, lat, run, sp, st, *scratch):
    w = Where(dims)
    hal, gat, ch = scratch[:6], scratch[6:9], scratch[9:16]
    col_s, col_r, cor_s, cor_r, hs, hr = hal
    buf, gs, gr = gat
    off = ch[4]
    cor_s[...] = jnp.zeros_like(cor_s)

    def clear(i, _):
        for k in range(T):
            sp[k, i] = jnp.zeros((PW, C), F32)
        return 0

    lax.fori_loop(0, HP, clear, 0)
    greet(w.tiles() + w.line())
    total = run.at[T - 1]
    chain_start(w, total, ch, False)
    for _ in chain_steps(w, total, ch, False):
        pass

    def fill(i, _):
        base = lat[i]
        o = off[i]
        sp[0, i + 1, 0:W, :] = base + o
        for k in range(1, T):
            sp[k, i + 1, 0:W, :] = base + (o + run[k - 1, i])
        return 0

    lax.fori_loop(0, H, fill, 0, unroll=2)
    halo_pack(sp, T, col_s, cor_s)
    copies = halo_copies(w, sp, col_s, col_r, cor_s, cor_r, hs, hr)
    for cp in copies:
        cp.start()
    means, devs = tile_moments(lambda f, i: sp[f, i + 1, 0:W, :], T)
    buf[w.me] = jnp.concatenate(means + devs, axis=0)
    sent = gather_start(w, buf, gs, gr)
    gather_wait(w, buf, gs, gr, sent)
    center, inv = moments(buf, w)
    st[0:T] = center
    st[T:] = inv
    for cp in copies:
        cp.wait()
    halo_unpack(sp, T, col_r, cor_r)


def k_adjoint(dims, coef, lat, rg, sp, st, dn, cs_in, run, traj, adj, suf, *scratch):
    w = Where(dims)
    gat, c1, c2 = scratch[:3], scratch[3:10], scratch[10:17]
    buf, gs, gr = gat
    buf[w.me] = cs_in[...]
    greet(w.tiles() + w.line())
    sent = gather_start(w, buf, gs, gr)
    chain_start(w, run.at[T - 1], c2, False)
    gather_wait(w, buf, gs, gr, sent)
    sums = jnp.sum(buf[...], axis=0)
    means = jnp.dot(sums, group_matrix(), precision=HI, preferred_element_type=F32)
    means = means * (1.0 / (H * W * w.nd * GSIZE))

    def row(i, _):
        rgv = rg[i]
        acc = None
        for k in range(T - 1, -1, -1):
            center, inv = st[k : k + 1, :], st[T + k : T + k + 1, :]
            plain, cross = means[k : k + 1, :], means[T + k : T + k + 1, :]
            norm = (sp[k, i + 1, 0:W, :] - center) * inv
            d = (dn[k, i] - plain - norm * cross) * inv
            t = coef[0, k] * rgv + (coef[1, k] * rgv + d)
            acc = t if acc is None else acc + t
            suf[k, i] = acc
        return 0

    lax.fori_loop(0, H, row, 0)
    total = suf.at[0]
    chain_start(w, total, c1, True)
    for _ in itertools.chain(
        chain_steps(w, total, c1, True), chain_steps(w, run.at[T - 1], c2, False)
    ):
        pass
    off1, off2 = c1[4], c2[4]

    def fin(i, _):
        o1, o2, base = off1[i], off2[i], lat[i]
        for k in range(T):
            adj[k, i] = o1 + suf[k + 1, i] if k + 1 < T else o1
            traj[k, i] = base + (o2 + run[k, i])
        return 0

    lax.fori_loop(0, H, fin, 0)


def k_reduce(dims, g, out, ra, s, ry, rz, s1, rz1, ry1, s2, rx, *sems):
    w = Where(dims)
    chips = w.nt // 2
    c = lax.rem(w.tm, 2)
    xme = lax.div(w.tm, 2)
    ny, nx = w.ny, w.nx
    sa, sb, sc_, sd, se = sems[0::2]
    qa, qb, qc, qd, qe = sems[1::2]
    partner = w.line()[0]

    def chip(d):
        q = lax.rem(xme + d, chips)
        return q, w.dev(2 * q + c, w.y, w.x)

    greet(w.tiles() + [partner] + [chip(d)[1] for d in range(1, chips)])
    done = []

    def go(cp):
        cp.start()
        done.append(cp)

    go(rcopy(g.at[:, 1 - c], ra, sa.at[0], qa.at[0], partner))
    done[-1].wait_recv()
    for x in range(chips):

        def add(i, _, x=x):
            for j in range(nx):
                s[x, i, j] = g[x, c, i, j] + ra[x, i, j]
            return 0

        lax.fori_loop(0, ny, add, 0)
    for d in range(1, nx):
        q = lax.rem(w.x + d, nx)
        go(rcopy(s.at[:, :, q, 0:4], rz.at[w.x], sb.at[d], qb.at[w.x], w.shift(0, d)))
    for d in range(1, ny):
        q = lax.rem(w.y + d, ny)
        go(rcopy(s.at[:, q, :, 4:8], ry.at[w.y], sb.at[nx + d], qb.at[nx + w.y], w.shift(d, 0)))
    for d in range(1, nx):
        q = lax.rem(w.x + d, nx)
        rcopy(rz.at[q], rz.at[q], sb.at[d], qb.at[q], partner).wait_recv()
    for d in range(1, ny):
        q = lax.rem(w.y + d, ny)
        rcopy(ry.at[q], ry.at[q], sb.at[nx + d], qb.at[nx + q], partner).wait_recv()
    for x in range(chips):
        for i in range(ny):
            acc = s[x, i, w.x, 0:4]
            for d in range(1, nx):
                acc += rz[lax.rem(w.x + d, nx), x, i]
            s1[0, x, i] = acc
        for j in range(nx):
            acc = s[x, w.y, j, 4:8]
            for d in range(1, ny):
                acc += ry[lax.rem(w.y + d, ny), x, j]
            s1[1, x, j] = acc
    for d in range(1, ny):
        q = lax.rem(w.y + d, ny)
        go(rcopy(s1.at[0, :, q], rz1.at[w.y], sc_.at[d], qc.at[w.y], w.shift(d, 0)))
    for d in range(1, nx):
        q = lax.rem(w.x + d, nx)
        go(rcopy(s1.at[1, :, q], ry1.at[w.x], sc_.at[ny + d], qc.at[ny + w.x], w.shift(0, d)))
    for d in range(1, ny):
        q = lax.rem(w.y + d, ny)
        rcopy(rz1.at[q], rz1.at[q], sc_.at[d], qc.at[q], partner).wait_recv()
    for d in range(1, nx):
        q = lax.rem(w.x + d, nx)
        rcopy(ry1.at[q], ry1.at[q], sc_.at[ny + d], qc.at[ny + q], partner).wait_recv()
    for x in range(chips):
        acc = s1[0, x, w.y]
        for d in range(1, ny):
            acc += rz1[lax.rem(w.y + d, ny), x]
        s2[x, 0:4] = acc
        acc = s1[1, x, w.x]
        for d in range(1, nx):
            acc += ry1[lax.rem(w.x + d, nx), x]
        s2[x, 4:8] = acc
    for d in range(1, chips):
        q, dev = chip(d)
        go(rcopy(s2.at[q], rx.at[xme], sd.at[d], qd.at[xme], dev))
    for d in range(1, chips):
        q, dev = chip(d)
        rcopy(rx.at[q], rx.at[q], sd.at[d], qd.at[q], dev).wait_recv()
    acc = s2[xme]
    for d in range(1, chips):
        acc += rx[lax.rem(xme + d, chips)]
    out[w.me] = acc
    sent = gather_start(w, out, se, qe)
    gather_wait(w, out, se, qe, sent)
    for cp in done:
        cp.wait_send()


def call(kernel, dims, args, outs, scratch, cid=None, smem=0):
    params = dict(vmem_limit_bytes=VLIM)
    if cid is not None:
        params.update(collective_id=cid, has_side_effects=True)
    return pl.pallas_call(
        functools.partial(kernel, dims),
        out_shape=tuple(jax.ShapeDtypeStruct(s, d) for s, d in outs),
        in_specs=[SM] * smem + [VM] * (len(args) - smem),
        out_specs=tuple(VM for _ in outs),
        scratch_shapes=scratch,
        compiler_params=pltpu.CompilerParams(**params),
        name=kernel.__name__,
    )(*args)


def pack_weight(wt):
    main = wt[:, :, 0:256].reshape(3, 768, C)
    tail = wt[:, :, 256:C].reshape(3, 192, C)
    return jnp.concatenate([main, tail, jnp.zeros((3, 64, C), wt.dtype)], axis=1)


def shards(dims, latent, noise, coef_state, coef_drift, coef_noise, step_index, table, gain, weight, rg):
    nt, ny, nx = dims
    nd = ny * nx
    ids = jnp.arange(table.shape[0], dtype=jnp.int32)
    hot = (step_index[:, None] == ids[None, :]).astype(F32)
    mod = gain[None, :] * (1.0 + jnp.dot(hot, table, precision=HI))
    coef = jnp.stack([coef_state, coef_drift, coef_noise])
    wr = pack_weight(weight)
    wd = pack_weight(jnp.transpose(weight[::-1, ::-1], (0, 1, 3, 2)))
    field = (T, H, W, C)
    abs_ = (T, HP, W, AW)
    p, st = call(
        k_open, dims, (latent, rg), [((2, HP, PW, C), F32), ((8, C), F32)],
        halo_scratch(2) + gather_scratch(nd), cid=0,
    )
    run, ab1, dact = call(
        k_first, dims, (coef, p, st, mod, wr, wd, noise),
        [(field, F32), (abs_, BF16), (field, F32)], [pltpu.VMEM(abs_, BF16)], smem=1,
    )
    sp, st2 = call(
        k_states, dims, (latent, run), [((T, HP, PW, C), F32), ((8, C), F32)],
        halo_scratch(T) + gather_scratch(nd) + chain_scratch(), cid=1,
    )
    run2, ab2, dn, cs = call(
        k_second, dims, (coef, sp, st2, mod, wr, noise, dact),
        [(field, F32), (abs_, BF16), (field, F32), ((8, C), F32)], [], smem=1,
    )
    traj, adj = call(
        k_adjoint, dims, (coef, latent, rg, sp, st2, dn, cs, run2),
        [(field, F32), (field, F32)],
        [pltpu.VMEM(field, F32)] + gather_scratch(nd) + chain_scratch() + chain_scratch(),
        cid=2, smem=1,
    )
    (g,) = call(
        k_weight, dims, (coef, rg, adj, ab1, ab2), [((nt, 128, 8, 128), F32)],
        [pltpu.VMEM((C, 2 * T * H * W), BF16)], smem=1,
    )
    chips = nt // 2
    per = 128 // nd
    dma = pltpu.SemaphoreType.DMA
    (out,) = call(
        k_reduce, dims, (g.reshape(chips, 2, ny, nx, per, 8, 128),), [((nd, per, 8, 128), F32)],
        [
            pltpu.VMEM((chips, ny, nx, per, 8, 128), F32),
            pltpu.VMEM((chips, ny, nx, per, 8, 128), F32),
            pltpu.VMEM((ny, chips, nx, per // 2, 8, 128), F32),
            pltpu.VMEM((nx, chips, ny, per // 2, 8, 128), F32),
            pltpu.VMEM((2, chips, 4, per // 2, 8, 128), F32),
            pltpu.VMEM((ny, chips, per // 2, 8, 128), F32),
            pltpu.VMEM((nx, chips, per // 2, 8, 128), F32),
            pltpu.VMEM((chips, per, 8, 128), F32),
            pltpu.VMEM((chips, per, 8, 128), F32),
            dma((1,)), dma((1,)),
            dma((nx + ny,)), dma((nx + ny,)),
            dma((nx + ny,)), dma((nx + ny,)),
            dma((chips,)), dma((chips,)),
            dma((nd,)), dma((nd,)),
        ],
        cid=3,
    )
    tiles = out.reshape(128, 8, 128)[:120].reshape(3, 8, 40, 128)
    flat = jnp.transpose(tiles, (0, 2, 1, 3)).reshape(3, 40, AW)
    main = flat[:, :, 0:768].reshape(3, 40, 3, 256)
    tail = flat[:, :, 768:960].reshape(3, 40, 3, 64)
    grad = jnp.transpose(jnp.concatenate([main, tail], axis=3), (0, 2, 3, 1))
    return traj, grad


def solution(mesh):
    dims = (mesh.shape["tm"], mesh.shape["sy"], mesh.shape["sx"])
    tile = P("sy", "sx", None)
    full = P("tm", "sy", "sx", None)
    step = P("tm")
    return jax.shard_map(
        functools.partial(shards, dims),
        mesh=mesh,
        in_specs=(tile, full, step, step, step, step, P(), P(), P(), tile),
        out_specs=(full, P(None, None, None, "tm")),
        check_vma=False,
    )
```

time: 641 us -> 222 us (0.35)
  Pallas kernels: 0 us -> 198 us
  blocking collectives: 192 us -> 0 us
  waiting for transfers between devices: 170 us -> 0 us
  matrix products: 101 us -> 1.98 us
  other arithmetic: 78.3 us -> 7.19 us
  local copies, waits for them, and re-layouts: 53.7 us -> 13.2 us
  starting transfers between devices: 24.5 us -> 0 us
  between operations: 15.5 us -> 0.77 us
    pallas_call x0 -> x7, Pallas kernels: none -> 198 us  [call(): pl.pallas_call(functools.partial(kernel, dims), out_shape=tuple((jax.Shap...]
    psum x5 -> x0, blocking collectives: 192 us -> none  [the longest x2 81.4 us: group_stats(): totals = lax.psum(jnp.sum(grouped, axis=(1, 3)), ('sy', 'sx'))]
    dot_general x46 -> x1, matrix products: 101 us -> 1.98 us  [shards(): mod = gain[None, :] * (1.0 + jnp.dot(hot, table, precision=HI))]
    psum x1 -> x0, waiting for transfers between devices: 77.7 us -> none  [shards(): grad_weight = lax.psum(share, ('sy', 'sx'))]
    unnamed x6 -> x0, waiting for transfers between devices: 51.2 us -> none
    all_gather x3 -> x0, waiting for transfers between devices: 33.7 us -> none  [prefix(): pieces = lax.all_gather(value, axis)]
    select_n x21 -> x0, other arithmetic: 25.6 us -> none  [step(): return jnp.where(position < mine, longer, subtotal)]
    ppermute x12 -> x0, starting transfers between devices: 24.1 us -> none  [the longest x6 16 us: with_halo(): lax.ppermute(lax.slice_in_dim(block, block.shape[dim] - width, None, axis...]
  transfers between devices with their start and end apart: 17 -> 0, of which waited for: 6 -> 0; matrix products, arithmetic and copies ran while one was open for 17% -> 0% of each run, Pallas kernels for 0% -> 0%
where the time goes in v1:
time: 222 us; the launch traced here: 221 us
  Pallas kernels  198 us (89%)
  local copies, waits for them, and re-layouts  13.2 us (6%)
  other arithmetic  7.19 us (3%)
    pallas_call x7, Pallas kernels, call(): pl.pallas_call(functools.partial(kernel, dims), out_shape=tuple((jax.Shap...  198 us
    concatenate x1, other arithmetic, pack_weight(): jnp.concatenate([main, tail, jnp.zeros((3, 64, C), wt.dtype)], axis=1)  5.67 us
    slice x4, local copies, waits for them, and re-layouts, pack_weight(): main = wt[:, :, 0:256].reshape(3, 768, C)  4.93 us

profile of v1, /device:TPU:0, one launch (start us, length us, event | category | flops | bytes accessed | tf_op | source)
XLA Modules:
  0.0 221.3 jit_solution(1030122187892828027)
XLA Ops:
  0.7 1.3 pad_maximum_fusion.coef
  2.1 2.0 fusion.mod
  4.1 17.1 %k_open.1 = (f32[2,18,32,320]{3,2,1,0:T(8,128)}, f32[8,320]{1,0:T(8,128)}) custom-call(f32[16,24,320]{2,1,0:T(8,128)} %lat.5, f32[16,24,320]{2,1,0:T(8,128)} %rg.5), custom_call_target="tpu_custom_call" | custom-call | tf_op jit(solution)/shard_map/k_open/pallas_call | solution.py:636
  21.1 0.2 reverse_bitcast_fusion
  21.4 1.0 slice.30
  22.4 1.2 slice.29
  23.6 2.3 %copy.15 = bf16[3,3,64,320]{3,2,1,0:T(8,128)(2,1)} copy(bf16[3,3,64,320]{2,3,1,0:T(8,128)(2,1)} %slice.30) | data formatting | bytes 737280 | tf_op jit(solution)/shard_map/slice | solution.py:649
  25.9 3.7 %copy.14 = bf16[3,3,256,320]{3,2,1,0:T(8,128)(2,1)} copy(bf16[3,3,256,320]{2,3,1,0:T(8,128)(2,1)} %slice.29) | data formatting | bytes 2949120 | tf_op jit(solution)/shard_map/slice | solution.py:648
  29.6 5.7 %maximum_maximum_fusion.1 = (bf16[3,1024,320]{2,1,0:T(8,128)(2,1)}, bf16[3,1024,320]{2,1,0:T(8,128)(2,1)}) fusion(bf16[3,192,320]{2,1,0:T(8,128)(2,1)} %bitcast.25, bf16[3,768,320]{2,1,0:T(8,128)(2,1)} %bitcast.22, bf16[1024]{0:T(1024)(128)(2,1)S(1)} %pad.7.clone, bf16[3,192,320]{2,1,0:T(8,128)(2,1)S(1)} %bitcast.20, bf16[3,768,320]{2,1,0:T(8,128)(2,1)S(1)} %bitcast.21), kind=kLoop, calls=%fused_computation.1 | loop fusion | flops 10813440 | bytes 7620608 | tf_op jit(solution)/shard_map/concatenate | solution.py:650
  35.3 22.8 %k_first.1 = (f32[4,16,24,320]{3,2,1,0:T(8,128)}, bf16[4,18,24,1024]{3,2,1,0:T(8,128)(2,1)}, f32[4,16,24,320]{3,2,1,0:T(8,128)}) custom-call(f32[3,4]{1,0:T(4,128)} %pad_maximum_fusion.coef, f32[2,18,32,320]{3,2,1,0:T(8,128)} %get-tuple-element.15.p, f32[8,320]{1,0:T(8,128)} %get-tuple-element.16.st, f32[4,320]{1,0:T(4,128)} %fusion.mod, ...), custom_call_target="tpu_custom_call" | custom-call | tf_op jit(solution)/shard_map/k_first/pallas_call | solution.py:636
  58.1 24.7 %k_states.1 = (f32[4,18,32,320]{3,2,1,0:T(8,128)}, f32[8,320]{1,0:T(8,128)}) custom-call(f32[16,24,320]{2,1,0:T(8,128)} %lat.5, f32[4,16,24,320]{3,2,1,0:T(8,128)} %get-tuple-element.17.run), custom_call_target="tpu_custom_call" | custom-call | tf_op jit(solution)/shard_map/k_states/pallas_call | solution.py:636
  82.8 18.5 %k_second.1 = (f32[4,16,24,320]{3,2,1,0:T(8,128)}, bf16[4,18,24,1024]{3,2,1,0:T(8,128)(2,1)}, f32[4,16,24,320]{3,2,1,0:T(8,128)}, f32[8,320]{1,0:T(8,128)}) custom-call(f32[3,4]{1,0:T(4,128)} %pad_maximum_fusion.coef, f32[4,18,32,320]{3,2,1,0:T(8,128)} %get-tuple-element.18.p.sp, f32[8,320]{1,0:T(8,128)} %get-tuple-element.19.st, f32[4,320]{1,0:T(4,128)} %fusion.mod, ...), custom_call_target="tpu_custom_call" | custom-call | tf_op jit(solution)/shard_map/k_second/pallas_call | solution.py:636
  101.3 51.3 %k_adjoint.1 = (f32[4,16,24,320]{3,2,1,0:T(8,128)}, f32[4,16,24,320]{3,2,1,0:T(8,128)}) custom-call(f32[3,4]{1,0:T(4,128)} %pad_maximum_fusion.coef, f32[16,24,320]{2,1,0:T(8,128)} %lat.5, f32[16,24,320]{2,1,0:T(8,128)} %rg.5, f32[4,18,32,320]{3,2,1,0:T(8,128)} %get-tuple-element.18.p.sp, f32[8,320]{1,0:T(8,128)} %get-tuple-element.19.st, ...), custom_call_target="tpu_custom_call" | custom-call | tf_op jit(solution)/shard_map/k_adjoint/pallas_call | solution.py:636
  152.6 12.2 %k_weight.1 = f32[8,128,8,128]{3,2,1,0:T(8,128)} custom-call(f32[3,4]{1,0:T(4,128)} %pad_maximum_fusion.coef, f32[16,24,320]{2,1,0:T(8,128)} %rg.5, f32[4,16,24,320]{3,2,1,0:T(8,128)} %get-tuple-element.25.adj, bf16[4,18,24,1024]{3,2,1,0:T(8,128)(2,1)} %get-tuple-element.26.ab1, bf16[4,18,24,1024]{3,2,1,0:T(8,128)(2,1)} %get-tuple-element.27.ab2), custom_call_target="tpu_custom_call" | custom-call | tf_op jit(solution)/shard_map/k_weight/pallas_call | solution.py:636
  164.8 51.6 %k_reduce.1 = f32[16,8,8,128]{3,2,1,0:T(8,128)} custom-call(f32[4,2,4,4,8,8,128]{6,5,4,3,2,1,0:T(8,128)} %bitcast.19), custom_call_target="tpu_custom_call" | custom-call | tf_op jit(solution)/shard_map/k_reduce/pallas_call | solution.py:636
  216.4 1.1 slice.26
  217.4 0.1 copy.19
  217.5 0.1 reshape.42
  217.7 0.2 reshape.43
  217.9 0.1 reshape.44
  218.0 0.2 maximum_bitcast_fusion
  218.2 0.8 copy.17
  219.0 0.8 copy-done.2
  219.9 1.4 copy.21
  (13 shorter events, 0.1 us)
Async XLA Ops:
  0.6 1.4 copy-start
  4.1 17.1 %copy-start.1 = (bf16[3,3,320,320]{3,2,1,0:T(8,128)(2,1)S(1)}, bf16[3,3,320,320]{3,2,1,0:T(8,128)(2,1)}, u32[]{:S(2)}) copy-start(bf16[3,3,320,320]{3,2,1,0:T(8,128)(2,1)} %param.18) | copy-start | bytes 5529604
  23.6 6.0 %slice-start = ((bf16[3,3,320,320]{3,2,1,0:T(8,128)(2,1)}), bf16[3,3,64,320]{3,2,1,0:T(8,128)(2,1)S(1)}, s32[]{:S(2)}) async-start(bf16[3,3,320,320]{3,2,1,0:T(8,128)(2,1)} %param.18), calls=%async_computation | async-start | bytes 884736 | tf_op jit(solution)/shard_map/slice | solution.py:649
  23.6 6.0 %slice-start.1 = ((bf16[3,3,320,320]{3,2,1,0:T(8,128)(2,1)}), bf16[3,3,256,320]{3,2,1,0:T(8,128)(2,1)S(1)}, s32[]{:S(2)}) async-start(bf16[3,3,320,320]{3,2,1,0:T(8,128)(2,1)} %param.18), calls=%async_computation.1 | async-start | bytes 3538944 | tf_op jit(solution)/shard_map/slice | solution.py:648
  218.0 1.9 copy-start.2

commit v2 on v1

v2 whole, which is shorter than its diff:
```python
import functools

import jax
import jax.numpy as jnp
from jax import lax
from jax.experimental import pallas as pl
from jax.experimental.pallas import tpu as pltpu
from jax.sharding import PartitionSpec as P

MESH = pl.DeviceIdType.MESH
VM = pl.BlockSpec(memory_space=pltpu.VMEM)
SM = pl.BlockSpec(memory_space=pltpu.SMEM)
F32 = jnp.float32
BF16 = jnp.bfloat16
HI = lax.Precision.HIGHEST
EPSILON = 1e-05
GSIZE = 10
T = 4
H = 16
W = 24
C = 320
PW = 32
HP = H + 2
AW = 1024
VLIM = 60 << 20


def rcopy(src, dst, ssem, rsem, dev):
    return pltpu.make_async_remote_copy(
        src_ref=src, dst_ref=dst, send_sem=ssem, recv_sem=rsem, device_id=dev, device_id_type=MESH
    )


def greet(devs):
    sem = pltpu.get_barrier_semaphore()
    for dev in devs:
        pl.semaphore_signal(sem, inc=1, device_id=dev, device_id_type=MESH)


class Where:
    def __init__(self, dims):
        self.nt, self.ny, self.nx = dims
        self.tm = lax.axis_index("tm")
        self.y = lax.axis_index("sy")
        self.x = lax.axis_index("sx")
        self.nd = self.ny * self.nx
        self.me = self.y * self.nx + self.x

    def dev(self, tm, y, x):
        return (tm, y, x)

    def tile(self, d):
        q = lax.rem(self.me + d, self.nd)
        return q, self.dev(self.tm, lax.div(q, self.nx), lax.rem(q, self.nx))

    def shift(self, dy, dx):
        return self.dev(
            self.tm,
            lax.rem(self.y + dy + self.ny, self.ny),
            lax.rem(self.x + dx + self.nx, self.nx),
        )

    def tiles(self):
        return [self.tile(d)[1] for d in range(1, self.nd)]

    def line(self):
        c = lax.rem(self.tm, 2)
        return [
            self.dev(self.tm + 1 - 2 * c, self.y, self.x),
            self.dev(lax.rem(self.tm + 2, self.nt), self.y, self.x),
            self.dev(lax.rem(self.tm + self.nt - 2, self.nt), self.y, self.x),
        ]


def gather_start(w, buf, ssem, rsem):
    out = []
    for d in range(1, w.nd):
        _, dev = w.tile(d)
        cp = rcopy(buf.at[w.me], buf.at[w.me], ssem.at[d], rsem.at[w.me], dev)
        cp.start()
        out.append(cp)
    return out


def gather_wait(w, buf, ssem, rsem, sent):
    for cp in sent:
        cp.wait_send()
    for d in range(1, w.nd):
        q, dev = w.tile(d)
        rcopy(buf.at[q], buf.at[q], ssem.at[d], rsem.at[q], dev).wait_recv()


def group_matrix():
    row = lax.broadcasted_iota(jnp.int32, (C, C), 0)
    col = lax.broadcasted_iota(jnp.int32, (C, C), 1)
    same = ((row * 6554) >> 16) == ((col * 6554) >> 16)
    return same.astype(F32)


def moments(buf, w):
    gm = group_matrix()
    n = float(H * W)
    both = buf[...]
    mean = jnp.sum(both[:, 0:T], axis=0) * (1.0 / w.nd)
    center = jnp.dot(mean, gm, precision=HI, preferred_element_type=F32) * (1.0 / GSIZE)
    off = both[:, 0:T] - center[None]
    dev = jnp.sum(both[:, T:] + n * off * off, axis=0)
    total = jnp.dot(dev, gm, precision=HI, preferred_element_type=F32)
    spread = total * (1.0 / (n * w.nd * GSIZE))
    return center, 1.0 / jnp.sqrt(spread + EPSILON)


SIDES = ((0, -1), (0, 1), (-1, 0), (1, 0), (-1, -1), (-1, 1), (1, -1), (1, 1))


def halo_pack(p, n, col_s, cor_s):
    for f in range(n):
        col_s[0, f] = p[f, 1 : 1 + H, 0, :]
        col_s[1, f] = p[f, 1 : 1 + H, W - 1, :]
        for j, (dy, dx) in enumerate(SIDES[4:]):
            row = 1 if dy < 0 else H
            lane = 0 if dx < 0 else W - 1
            cor_s[j, f : f + 1, :] = p[f, row, lane : lane + 1, :]


def halo_copies(w, p, col_s, col_r, cor_s, cor_r, ssem, rsem):
    out = []
    for j, (dy, dx) in enumerate(SIDES):
        dev = w.shift(dy, dx)
        if j < 2:
            src, dst = col_s.at[j], col_r.at[j]
        elif j < 4:
            row, land = (1, HP - 1) if dy < 0 else (H, 0)
            src, dst = p.at[:, row, 0:W, :], p.at[:, land, 0:W, :]
        else:
            src, dst = cor_s.at[j - 4], cor_r.at[j - 4]
        out.append(rcopy(src, dst, ssem.at[j], rsem.at[j], dev))
    return out


def halo_unpack(p, n, col_r, cor_r):
    for f in range(n):
        p[f, 1 : 1 + H, W, :] = col_r[0, f]
        p[f, 1 : 1 + H, PW - 1, :] = col_r[1, f]
        for j, (dy, dx) in enumerate(SIDES[4:]):
            row = HP - 1 if dy < 0 else 0
            lane = W if dx < 0 else PW - 1
            p[f, row, lane : lane + 1, :] = cor_r[j, f : f + 1, :]


def halo_scratch(n):
    return [
        pltpu.VMEM((2, n, H, C), F32),
        pltpu.VMEM((2, n, H, C), F32),
        pltpu.VMEM((4, 8, C), F32),
        pltpu.VMEM((4, 8, C), F32),
        pltpu.SemaphoreType.DMA((8,)),
        pltpu.SemaphoreType.DMA((8,)),
    ]


def gather_scratch(nd):
    return [
        pltpu.VMEM((nd, 8, C), F32),
        pltpu.SemaphoreType.DMA((nd,)),
        pltpu.SemaphoreType.DMA((nd,)),
    ]


def tile_moments(read, n):
    cells = 1.0 / (H * W)
    means, devs = [], []
    for f in range(n):

        def add(i, acc, f=f):
            return acc + read(f, i)

        total = lax.fori_loop(0, H, add, jnp.zeros((W, C), F32), unroll=4)
        mean = jnp.sum(total, axis=0, keepdims=True) * cells

        def add2(i, acc, f=f, mean=mean):
            v = read(f, i) - mean
            return acc + v * v

        total = lax.fori_loop(0, H, add2, jnp.zeros((W, C), F32), unroll=4)
        means.append(mean)
        devs.append(jnp.sum(total, axis=0, keepdims=True))
    return means, devs


CH = 4
ROWS = H // CH


def edge_mask(w, i):
    col = lax.broadcasted_iota(jnp.int32, (PW, 1), 0)
    rows = jnp.logical_and(
        jnp.logical_or(i > 0, w.y > 0), jnp.logical_or(i < HP - 1, w.y < w.ny - 1)
    )
    left = jnp.where(w.x > 0, 1, 0)
    right = jnp.where(w.x < w.nx - 1, 1, 0)
    inside = jnp.where(col == PW - 1, left, jnp.where(col == W, right, 1))
    return inside * jnp.where(rows, 1, 0) > 0


def pack_row(ab, k, i, v):
    shifts = [pltpu.roll(v, 1, 0)[0:W], v[0:W], pltpu.roll(v, PW - 1, 0)[0:W]]
    for s in range(3):
        ab[k, i, :, 256 * s : 256 * s + 256] = shifts[s][:, 0:256].astype(BF16)
    tail = jnp.concatenate(
        [u[:, 256:C] for u in shifts] + [jnp.zeros((W, 64), F32)], axis=1
    )
    ab[k, i, :, 768:AW] = tail.astype(BF16)


def conv_rows(ab, j, wt):
    acc = None
    for r in range(3):
        lhs = ab[:, pl.ds(ROWS * j + r, ROWS)].reshape(T * ROWS * W, AW)
        out = jnp.dot(lhs, wt[r], preferred_element_type=F32)
        acc = out if acc is None else acc + out
    return acc.reshape(T, ROWS, W, C)


def pack_weights(weight, wr, wd):
    for r in range(3):
        for dst in (wr, wd):
            dst[r, 960:AW] = jnp.zeros((64, C), BF16)
        for s in range(3):
            one = weight[r, s]
            wr[r, 256 * s : 256 * s + 256] = one[0:256]
            wr[r, 768 + 64 * s : 832 + 64 * s] = one[256:C]
            turned = weight[2 - r, 2 - s].T
            wd[r, 256 * s : 256 * s + 256] = turned[0:256]
            wd[r, 768 + 64 * s : 832 + 64 * s] = turned[256:C]


def build_act(w, p, field, st, mod, ab, k):
    center = st[pl.ds(k, 1), :]
    inv = st[pl.ds(T + k, 1), :]
    m = mod[pl.ds(k, 1), :]

    def row(i, _):
        pre = (p[field, i] - center) * inv * m
        act = pre / (1.0 + jnp.exp(-pre))
        act = jnp.where(edge_mask(w, i), act, 0.0)
        pack_row(ab, k, i, act)
        return 0

    lax.fori_loop(0, HP, row, 0, unroll=2)


def chain_scratch():
    part = (CH, ROWS // 2, W, C)
    return [
        pltpu.VMEM(part, F32),
        pltpu.VMEM(part, F32),
        pltpu.VMEM(part, F32),
        pltpu.VMEM(part, F32),
        pltpu.VMEM((H, W, C), F32),
        pltpu.SemaphoreType.DMA((3 * CH,)),
        pltpu.SemaphoreType.DMA((3 * CH,)),
    ]


class Chain:
    def __init__(self, w, total, scr, rev):
        self.w, self.total, self.scr = w, total, scr
        self.prx, self.inc, self.outc, self.offp, self.off, self.ss, self.rs = scr
        self.c = lax.rem(w.tm, 2)
        self.chips = w.nt // 2
        x = lax.div(w.tm, 2)
        self.partner, nxt, prv = w.line()
        self.nxt = prv if rev else nxt
        self.x = self.chips - 1 - x if rev else x
        self.second = (self.c == 0) if rev else (self.c == 1)

    def rows(self, j, c):
        hh = ROWS // 2
        return pl.ds(ROWS * j + hh * c, hh)

    def pair(self, j):
        return rcopy(
            self.total.at[self.rows(j, 1 - self.c)], self.prx.at[j], self.ss.at[j], self.rs.at[j], self.partner
        )

    def fwd(self, j):
        return rcopy(
            self.outc.at[j], self.inc.at[j], self.ss.at[CH + j], self.rs.at[CH + j], self.nxt
        )

    def give(self, j, c):
        return rcopy(
            self.offp.at[j], self.off.at[self.rows(j, c)],
            self.ss.at[2 * CH + j], self.rs.at[2 * CH + j], self.partner,
        )

    def step(self, j):
        self.pair(j).wait_recv()

        @pl.when(self.x == 0)
        def _():
            self.inc[j] = jnp.zeros((ROWS // 2, W, C), F32)

        @pl.when(self.x > 0)
        def _():
            self.fwd(j).wait_recv()

        mine = self.total[self.rows(j, self.c)]

        @pl.when(self.x < self.chips - 1)
        def _():
            self.outc[j] = self.inc[j] + (mine + self.prx[j])
            self.fwd(j).start()

        got = self.inc[j]
        self.off[self.rows(j, self.c)] = got + jnp.where(self.second, self.prx[j], 0.0)
        self.offp[j] = got + jnp.where(self.second, 0.0, mine)
        self.give(j, self.c).start()

    def steps(self):
        for j in range(CH):
            self.step(j)

    def finish(self):
        for j in range(CH):
            self.pair(j).wait_send()
            self.give(j, self.c).wait_send()
            self.give(j, 1 - self.c).wait_recv()

            @pl.when(self.x < self.chips - 1)
            def _(j=j):
                self.fwd(j).wait_send()


def wgrad(upt, ab, g, r, first):
    chips = g.shape[0]
    for j in range(AW // 256):
        rhs = [
            ab[k, pl.ds(r, H), :, 256 * j : 256 * j + 256].reshape(H * W, 256) for k in range(T)
        ]
        out = jnp.dot(upt[...], jnp.concatenate(rhs, axis=0), preferred_element_type=F32)
        for half in range(2):
            place = pl.ds(5 * (r * 8 + j * 2 + half), 5)
            part = out[:, 128 * half : 128 * half + 128].reshape(chips, 2, 5, 8, 128)
            g[:, :, place] = part if first else g[:, :, place] + part


def loop_where(count, cond, step):
    def one(j, _):
        @pl.when(cond(j))
        def _():
            step(j, 0)

        return 0

    lax.fori_loop(0, count, one, 0)


def k_all(dims, *refs):
    (index, cstate, cdrift, cnoise, lat, rg, noise, weight, table, gain) = refs[:10]
    traj, out = refs[10:12]
    (p, sp, run, run2, dact, ab1, ab2, abu, wr, wd, mod, st, st2, upt1, upt2) = refs[12:27]
    hal1, hal2 = refs[27:33], refs[33:39]
    gat1, gat2, gat3 = refs[39:42], refs[42:45], refs[45:48]
    ch1, ch2, ch3 = refs[48:55], refs[55:62], refs[62:69]
    g, ra, s, ry, rz, s1, rz1, ry1, s2, rx = refs[69:79]
    sems = refs[79:]
    sa, sb, sc_, sd, se = sems[0::2]
    qa, qb, qc, qd, qe = sems[1::2]
    w = Where(dims)
    chips = w.nt // 2
    c = lax.rem(w.tm, 2)
    xme = lax.div(w.tm, 2)
    ny, nx = w.ny, w.nx
    partner = w.line()[0]

    def chip(d):
        q = lax.rem(xme + d, chips)
        return q, w.dev(2 * q + c, w.y, w.x)

    devs = w.tiles() + [partner] + [chip(d)[1] for d in range(1, chips)]
    greet(devs)

    def fill(i, _):
        for f, ref in ((0, lat), (1, rg)):
            p[f, i + 1, 0:W, :] = ref[i]
        return 0

    lax.fori_loop(0, H, fill, 0)
    for hal in (hal1, hal2):
        hal[2][...] = jnp.zeros_like(hal[2])
    halo_pack(p, 2, hal1[0], hal1[2])
    means, vars_ = tile_moments(lambda f, i: lat[i], 1)
    gat1[0][w.me] = jnp.concatenate(means * T + vars_ * T, axis=0)
    pl.semaphore_wait(pltpu.get_barrier_semaphore(), len(devs))
    sent1 = gather_start(w, *gat1)
    copies1 = halo_copies(w, p, *hal1)
    for cp in copies1:
        cp.start()

    pack_weights(weight, wr, wd)
    for k in range(T):
        mod[k : k + 1, :] = gain[...] * (1.0 + table[pl.ds(index[k], 1), :])
    turned = rg[...].reshape(H * W, C).T
    for k in range(T):
        upt2[:, k * H * W : (k + 1) * H * W] = (cdrift[k] * turned).astype(BF16)
    g[:, :, 120:128] = jnp.zeros((chips, 2, 8, 8, 128), F32)
    for cp in copies1:
        cp.wait()
    halo_unpack(p, 2, hal1[1], hal1[3])

    def up_row(i, _):
        mask = edge_mask(w, i)
        v = jnp.where(mask, p[1, i], 0.0)
        for k in range(T):
            pack_row(abu, k, i, cdrift[k] * v)
        return 0

    lax.fori_loop(0, HP, up_row, 0)
    gather_wait(w, *gat1, sent1)
    center, inv = moments(gat1[0], w)
    st[0:T] = center
    st[T:] = inv

    def act1(k, _):
        build_act(w, p, 0, st, mod, ab1, k)
        return 0

    lax.fori_loop(0, T, act1, 0)
    chain1 = Chain(w, run.at[T - 1], ch1, False)
    chain3 = Chain(w, run2.at[T - 1], ch3, False)

    def sweep(field, ab, dst, j):
        conv = conv_rows(ab, j, wr)
        rows = pl.ds(ROWS * j, ROWS)
        acc = None
        for k in range(T):
            v = field(k, j)
            inc = cstate[k] * v + cdrift[k] * (v + conv[k])
            inc = inc + cnoise[k] * noise[k, rows].astype(F32)
            acc = inc if acc is None else acc + inc
            dst[k, rows] = acc

    for j in range(CH):
        sweep(lambda k, j: lat[pl.ds(ROWS * j, ROWS)], ab1, run, j)
        chain1.pair(j).start()

    def back(j, _):
        dact[:, pl.ds(ROWS * j, ROWS)] = conv_rows(abu, j, wd)
        return 0

    early = jnp.clip(2 * (xme - 1), 0, CH)
    loop_where(CH, lambda j: j < early, back)
    chain1.steps()
    chain1.finish()

    def states(i, _):
        base = lat[i]
        o = chain1.off[i]
        sp[0, i + 1, 0:W, :] = base + o
        for k in range(1, T):
            sp[k, i + 1, 0:W, :] = base + (o + run[k - 1, i])
        return 0

    lax.fori_loop(0, H, states, 0, unroll=2)
    halo_pack(sp, T, hal2[0], hal2[2])
    copies2 = halo_copies(w, sp, *hal2)
    for cp in copies2:
        cp.start()
    means, vars_ = tile_moments(lambda f, i: sp[f, i + 1, 0:W, :], T)
    gat2[0][w.me] = jnp.concatenate(means + vars_, axis=0)
    sent2 = gather_start(w, *gat2)
    loop_where(CH, lambda j: j >= early, back)
    gather_wait(w, *gat2, sent2)
    center, inv = moments(gat2[0], w)
    st2[0:T] = center
    st2[T:] = inv

    sums = []
    for k in range(T):
        center, inv, m = st2[k : k + 1, :], st2[T + k : T + k + 1, :], mod[k : k + 1, :]

        def dnorm(i, acc, k=k, center=center, inv=inv, m=m):
            plain, cross = acc
            norm = (sp[k, i + 1, 0:W, :] - center) * inv
            pre = norm * m
            sig = 1.0 / (1.0 + jnp.exp(-pre))
            d = dact[k, i] * sig * (1.0 + pre * (1.0 - sig)) * m
            dact[k, i] = d
            return plain + d, cross + d * norm

        zero = jnp.zeros((W, C), F32)
        plain, cross = lax.fori_loop(0, H, dnorm, (zero, zero), unroll=2)
        sums.append((jnp.sum(plain, axis=0, keepdims=True), jnp.sum(cross, axis=0, keepdims=True)))
    gat3[0][w.me] = jnp.concatenate([a for a, _ in sums] + [b for _, b in sums], axis=0)
    sent3 = gather_start(w, *gat3)
    for cp in copies2:
        cp.wait()
    halo_unpack(sp, T, hal2[1], hal2[3])

    def act2(k, _):
        build_act(w, sp, k, st2, mod, ab2, k)
        return 0

    lax.fori_loop(0, T, act2, 0)
    gather_wait(w, *gat3, sent3)
    sums = jnp.sum(gat3[0][...], axis=0)
    means = jnp.dot(sums, group_matrix(), precision=HI, preferred_element_type=F32)
    means = means * (1.0 / (H * W * w.nd * GSIZE))

    chain2 = Chain(w, run.at[0], ch2, True)

    def through(i, _):
        rgv = rg[i]
        acc = None
        for k in range(T - 1, -1, -1):
            center, inv = st2[k : k + 1, :], st2[T + k : T + k + 1, :]
            plain, cross = means[k : k + 1, :], means[T + k : T + k + 1, :]
            norm = (sp[k, i + 1, 0:W, :] - center) * inv
            d = (dact[k, i] - plain - norm * cross) * inv
            t = cstate[k] * rgv + (cdrift[k] * rgv + d)
            acc = t if acc is None else acc + t
            run[k, i] = acc
        return 0

    for j in range(CH):
        lax.fori_loop(0, ROWS, lambda i, z, j=j: through(ROWS * j + i, z), 0)
        chain2.pair(j).start()

    def second(j, _):
        sweep(lambda k, j: sp[k, pl.ds(1 + ROWS * j, ROWS), 0:W, :], ab2, run2, j)
        return 0

    def weight2(r, _):
        wgrad(upt2, ab2, g, r, True)
        return 0

    n = jnp.clip(2 * chain2.x, 0, CH)
    m = jnp.where(chain2.x == chips - 1, 3, 0)
    loop_where(CH, lambda j: j < n, second)
    loop_where(3, lambda r: r < m, weight2)
    chain2.steps()
    loop_where(CH, lambda j: j >= n, second)
    for j in range(CH):
        chain3.pair(j).start()
    loop_where(3, lambda r: r >= m, weight2)
    chain2.finish()

    for k in range(T):
        adj = chain2.off[...] + run[k + 1] if k + 1 < T else chain2.off[...]
        up = (cdrift[k] * adj).reshape(H * W, C).astype(BF16)
        upt1[:, k * H * W : (k + 1) * H * W] = up.T

    def pairs(r):
        place = pl.ds(40 * r, 40)
        return rcopy(g.at[:, 1 - c, place], ra.at[:, place], sa.at[r], qa.at[r], partner)

    for r in range(3):
        wgrad(upt1, ab1, g, r, False)
        pairs(r).start()
    done = []

    def go(cp):
        cp.start()
        done.append(cp)

    per = g.shape[2] // w.nd

    def add(q, _):
        place = pl.ds(per * q, per)
        for x in range(chips):
            s[x, lax.div(q, nx), lax.rem(q, nx)] = g[x, c, place] + ra[x, place]
        return 0

    for r in range(3):
        pairs(r).wait_recv()
        lax.fori_loop(5 * r, 5 * r + 5, add, 0)
    for x in range(chips):
        s[x, ny - 1, nx - 1] = jnp.zeros((per, 8, 128), F32)
    for d in range(1, nx):
        q = lax.rem(w.x + d, nx)
        go(rcopy(s.at[:, :, q, 0:4], rz.at[w.x], sb.at[d], qb.at[w.x], w.shift(0, d)))
    for d in range(1, ny):
        q = lax.rem(w.y + d, ny)
        go(rcopy(s.at[:, q, :, 4:8], ry.at[w.y], sb.at[nx + d], qb.at[nx + w.y], w.shift(d, 0)))
    chain3.steps()
    for d in range(1, nx):
        q = lax.rem(w.x + d, nx)
        rcopy(rz.at[q], rz.at[q], sb.at[d], qb.at[q], partner).wait_recv()
    for d in range(1, ny):
        q = lax.rem(w.y + d, ny)
        rcopy(ry.at[q], ry.at[q], sb.at[nx + d], qb.at[nx + q], partner).wait_recv()

    def join(x, _):
        for i in range(ny):
            acc = s[x, i, w.x, 0:4]
            for d in range(1, nx):
                acc += rz[lax.rem(w.x + d, nx), x, i]
            s1[0, x, i] = acc
        for j in range(nx):
            acc = s[x, w.y, j, 4:8]
            for d in range(1, ny):
                acc += ry[lax.rem(w.y + d, ny), x, j]
            s1[1, x, j] = acc
        return 0

    lax.fori_loop(0, chips, join, 0)
    for d in range(1, ny):
        q = lax.rem(w.y + d, ny)
        go(rcopy(s1.at[0, :, q], rz1.at[w.y], sc_.at[d], qc.at[w.y], w.shift(d, 0)))
    for d in range(1, nx):
        q = lax.rem(w.x + d, nx)
        go(rcopy(s1.at[1, :, q], ry1.at[w.x], sc_.at[ny + d], qc.at[ny + w.x], w.shift(0, d)))
    chain3.finish()

    def final(i, _):
        o2, base = chain3.off[i], lat[i]
        for k in range(T):
            traj[k, i] = base + (o2 + run2[k, i])
        return 0

    lax.fori_loop(0, H, final, 0)
    for d in range(1, ny):
        q = lax.rem(w.y + d, ny)
        rcopy(rz1.at[q], rz1.at[q], sc_.at[d], qc.at[q], partner).wait_recv()
    for d in range(1, nx):
        q = lax.rem(w.x + d, nx)
        rcopy(ry1.at[q], ry1.at[q], sc_.at[ny + d], qc.at[ny + q], partner).wait_recv()
    for x in range(chips):
        acc = s1[0, x, w.y]
        for d in range(1, ny):
            acc += rz1[lax.rem(w.y + d, ny), x]
        s2[x, 0:4] = acc
        acc = s1[1, x, w.x]
        for d in range(1, nx):
            acc += ry1[lax.rem(w.x + d, nx), x]
        s2[x, 4:8] = acc
    for d in range(1, chips):
        q, dev = chip(d)
        go(rcopy(s2.at[q], rx.at[xme], sd.at[d], qd.at[xme], dev))
    for d in range(1, chips):
        q, dev = chip(d)
        rcopy(rx.at[q], rx.at[q], sd.at[d], qd.at[q], dev).wait_recv()
    acc = s2[xme]
    for d in range(1, chips):
        acc += rx[lax.rem(xme + d, chips)]
    out[w.me] = acc
    sent = gather_start(w, out, se, qe)
    gather_wait(w, out, se, qe, sent)
    for r in range(3):
        pairs(r).wait_send()
    for cp in done:
        cp.wait_send()


def shards(dims, latent, noise, coef_state, coef_drift, coef_noise, step_index, table, gain, weight, rg):
    nt, ny, nx = dims
    nd = ny * nx
    chips = nt // 2
    per = 128 // nd
    half = per // 2
    dma = pltpu.SemaphoreType.DMA
    vmem = pltpu.VMEM
    field = (T, H, W, C)
    packed = (T, HP, W, AW)
    scratch = [
        vmem((2, HP, PW, C), F32),
        vmem((T, HP, PW, C), F32),
        vmem(field, F32),
        vmem(field, F32),
        vmem(field, F32),
        vmem(packed, BF16),
        vmem(packed, BF16),
        vmem(packed, BF16),
        vmem((3, AW, C), BF16),
        vmem((3, AW, C), BF16),
        vmem((T, C), F32),
        vmem((2 * T, C), F32),
        vmem((2 * T, C), F32),
        vmem((C, T * H * W), BF16),
        vmem((C, T * H * W), BF16),
    ]
    scratch += halo_scratch(2) + halo_scratch(T)
    scratch += gather_scratch(nd) * 3 + chain_scratch() * 3
    scratch += [
        vmem((chips, 2, 128, 8, 128), F32),
        vmem((chips, 128, 8, 128), F32),
        vmem((chips, ny, nx, per, 8, 128), F32),
        vmem((ny, chips, nx, half, 8, 128), F32),
        vmem((nx, chips, ny, half, 8, 128), F32),
        vmem((2, chips, max(nx, ny), half, 8, 128), F32),
        vmem((ny, chips, half, 8, 128), F32),
        vmem((nx, chips, half, 8, 128), F32),
        vmem((chips, per, 8, 128), F32),
        vmem((chips, per, 8, 128), F32),
    ]
    for count in (3, nx + ny, nx + ny, chips, nd):
        scratch += [dma((count,)), dma((count,))]
    traj, out = pl.pallas_call(
        functools.partial(k_all, dims),
        out_shape=(
            jax.ShapeDtypeStruct(field, F32),
            jax.ShapeDtypeStruct((nd, per, 8, 128), F32),
        ),
        in_specs=[SM] * 4 + [VM] * 6,
        out_specs=(VM, VM),
        scratch_shapes=scratch,
        compiler_params=pltpu.CompilerParams(
            vmem_limit_bytes=VLIM, collective_id=0, has_side_effects=True
        ),
        name="picard",
    )(step_index, coef_state, coef_drift, coef_noise, latent, rg, noise, weight, table, gain[None])
    tiles = out.reshape(128, 8, 128)[:120].reshape(3, 8, 40, 128)
    flat = jnp.transpose(tiles, (0, 2, 1, 3)).reshape(3, 40, AW)
    main = flat[:, :, 0:768].reshape(3, 40, 3, 256)
    tail = flat[:, :, 768:960].reshape(3, 40, 3, 64)
    grad = jnp.transpose(jnp.concatenate([main, tail], axis=3), (0, 2, 3, 1))
    return traj, grad


def solution(mesh):
    dims = (mesh.shape["tm"], mesh.shape["sy"], mesh.shape["sx"])
    tile = P("sy", "sx", None)
    full = P("tm", "sy", "sx", None)
    step = P("tm")
    return jax.shard_map(
        functools.partial(shards, dims),
        mesh=mesh,
        in_specs=(tile, full, step, step, step, step, P(), P(), P(), tile),
        out_specs=(full, P(None, None, None, "tm")),
        check_vma=False,
    )
```

time: 222 us -> 129 us (0.58)
  Pallas kernels: 198 us -> 119 us
  other arithmetic: 7.19 us -> 0.18 us
  local copies, waits for them, and re-layouts: 13.2 us -> 8.45 us
    pallas_call x7 -> x1, Pallas kernels: 198 us -> 119 us  [shards(): pl.pallas_call(functools.partial(k_all, dims), out_shape=(jax.ShapeDtypeS...]
    slice x8 -> x0, local copies, waits for them, and re-layouts: 8.24 us -> none  [the longest x4 4.93 us: pack_weight(): main = wt[:, :, 0:256].reshape(3, 768, C)]
    concatenate x1 -> x0, other arithmetic: 5.67 us -> none  [pack_weight(): jnp.concatenate([main, tail, jnp.zeros((3, 64, C), wt.dtype)], axis=1)]
    unnamed x8 -> x5, local copies, waits for them, and re-layouts: 3.09 us -> 5.62 us
where the time goes in v2:
time: 129 us; the launch traced here: 128 us
  Pallas kernels  119 us (92%)
  local copies, waits for them, and re-layouts  8.45 us (7%)
    pallas_call x1, Pallas kernels, shards(): pl.pallas_call(functools.partial(k_all, dims), out_shape=(jax.ShapeDtypeS...  119 us
    unnamed x5, local copies, waits for them, and re-layouts  5.62 us

profile of v2, /device:TPU:0, one launch (start us, length us, event | category | flops | bytes accessed | tf_op | source)
XLA Modules:
  0.0 128.5 jit_solution(2893781006481364140)
XLA Ops:
  0.6 1.2 broadcast_in_dim.3.refs_9_
  1.9 2.9 %copy.13.refs_8_ = f32[1000,320]{1,0:T(8,128)} copy(f32[1000,320]{0,1:T(8,128)} %param.16) | data formatting | bytes 2560000 | tf_op args[6]
  4.8 119.2 %picard.1 = (f32[4,16,24,320]{3,2,1,0:T(8,128)}, f32[16,8,8,128]{3,2,1,0:T(8,128)}) custom-call(s32[4]{0:T(128)} %refs_0_.1, f32[4]{0:T(128)} %refs_1_.1, f32[4]{0:T(128)} %refs_2_.1, f32[4]{0:T(128)} %refs_3_.1, f32[16,24,320]{2,1,0:T(8,128)} %refs_4_.1, f32[16,24,320]{2,1,0:T(8,128)} %refs_5_.1, bf16[4,16,24,320]{3,2,1,0:T(8,128)(2,1)} %refs_6_.1, ...), custom_call_target="tpu_custom_call" | custom-call | tf_op jit(solution)/shard_map/picard/pallas_call | solution.py:700
  123.9 1.1 slice.10
  125.0 0.1 copy.17
  125.1 0.1 reshape.20
  125.2 0.0 copy-start
  125.3 0.2 reshape.21
  125.5 0.1 reshape.22
  125.6 0.2 maximum_bitcast_fusion
  125.8 0.8 copy.15
  126.6 0.5 copy-done
  127.1 1.4 %copy.19 = f32[4,16,24,320]{3,2,1,0:T(8,128)} copy(f32[4,16,24,320]{3,2,1,0:T(8,128)S(1)} %copy-done) | data formatting | bytes 3932160
  (2 shorter events, 0.0 us)
Async XLA Ops:
  125.2 1.9 %copy-start = (f32[4,16,24,320]{3,2,1,0:T(8,128)S(1)}, f32[4,16,24,320]{3,2,1,0:T(8,128)}, u32[]{:S(2)}) copy-start(f32[4,16,24,320]{3,2,1,0:T(8,128)} %get-tuple-element.10) | copy-start | bytes 5898244

commit v3 on v2

--- a/solution.py
+++ b/solution.py
@@ -10,6 +10,7 @@
 MESH = pl.DeviceIdType.MESH
 VM = pl.BlockSpec(memory_space=pltpu.VMEM)
 SM = pl.BlockSpec(memory_space=pltpu.SMEM)
+ANY = pl.BlockSpec(memory_space=pl.ANY)
 F32 = jnp.float32
 BF16 = jnp.bfloat16
 HI = lax.Precision.HIGHEST
@@ -222,17 +223,22 @@
     return acc.reshape(T, ROWS, W, C)
 
 
-def pack_weights(weight, wr, wd):
+def pack_forward(weight, wr):
     for r in range(3):
-        for dst in (wr, wd):
-            dst[r, 960:AW] = jnp.zeros((64, C), BF16)
+        wr[r, 960:AW] = jnp.zeros((64, C), BF16)
         for s in range(3):
             one = weight[r, s]
             wr[r, 256 * s : 256 * s + 256] = one[0:256]
             wr[r, 768 + 64 * s : 832 + 64 * s] = one[256:C]
-            turned = weight[2 - r, 2 - s].T
-            wd[r, 256 * s : 256 * s + 256] = turned[0:256]
-            wd[r, 768 + 64 * s : 832 + 64 * s] = turned[256:C]
+
+
+def pack_backward(weight, wd):
+    for r in range(3):
+        wd[r, 960:AW] = jnp.zeros((64, C), BF16)
+        for s in range(3):
+            one = weight[2 - r, 2 - s].T
+            wd[r, 256 * s : 256 * s + 256] = one[0:256]
+            wd[r, 768 + 64 * s : 832 + 64 * s] = one[256:C]
 
 
 def build_act(w, p, field, st, mod, ab, k):
@@ -242,7 +248,7 @@
 
     def row(i, _):
         pre = (p[field, i] - center) * inv * m
-        act = pre / (1.0 + jnp.exp(-pre))
+        act = pre * (0.5 + 0.5 * jnp.tanh(0.5 * pre))
         act = jnp.where(edge_mask(w, i), act, 0.0)
         pack_row(ab, k, i, act)
         return 0
@@ -250,16 +256,16 @@
     lax.fori_loop(0, HP, row, 0, unroll=2)
 
 
-def chain_scratch():
-    part = (CH, ROWS // 2, W, C)
+def chain_scratch(count):
+    part = (count, H // count // 2, W, C)
     return [
         pltpu.VMEM(part, F32),
         pltpu.VMEM(part, F32),
         pltpu.VMEM(part, F32),
         pltpu.VMEM(part, F32),
         pltpu.VMEM((H, W, C), F32),
-        pltpu.SemaphoreType.DMA((3 * CH,)),
-        pltpu.SemaphoreType.DMA((3 * CH,)),
+        pltpu.SemaphoreType.DMA((3 * count,)),
+        pltpu.SemaphoreType.DMA((3 * count,)),
     ]
 
 
@@ -267,6 +273,8 @@
     def __init__(self, w, total, scr, rev):
         self.w, self.total, self.scr = w, total, scr
         self.prx, self.inc, self.outc, self.offp, self.off, self.ss, self.rs = scr
+        self.n = self.prx.shape[0]
+        self.per = H // self.n
         self.c = lax.rem(w.tm, 2)
         self.chips = w.nt // 2
         x = lax.div(w.tm, 2)
@@ -276,8 +284,8 @@
         self.second = (self.c == 0) if rev else (self.c == 1)
 
     def rows(self, j, c):
-        hh = ROWS // 2
-        return pl.ds(ROWS * j + hh * c, hh)
+        hh = self.per // 2
+        return pl.ds(self.per * j + hh * c, hh)
 
     def pair(self, j):
         return rcopy(
@@ -286,13 +294,13 @@
 
     def fwd(self, j):
         return rcopy(
-            self.outc.at[j], self.inc.at[j], self.ss.at[CH + j], self.rs.at[CH + j], self.nxt
+            self.outc.at[j], self.inc.at[j], self.ss.at[self.n + j], self.rs.at[self.n + j], self.nxt
         )
 
     def give(self, j, c):
         return rcopy(
             self.offp.at[j], self.off.at[self.rows(j, c)],
-            self.ss.at[2 * CH + j], self.rs.at[2 * CH + j], self.partner,
+            self.ss.at[2 * self.n + j], self.rs.at[2 * self.n + j], self.partner,
         )
 
     def step(self, j):
@@ -300,7 +308,7 @@
 
         @pl.when(self.x == 0)
         def _():
-            self.inc[j] = jnp.zeros((ROWS // 2, W, C), F32)
+            self.inc[j] = jnp.zeros((self.per // 2, W, C), F32)
 
         @pl.when(self.x > 0)
         def _():
@@ -318,12 +326,18 @@
         self.offp[j] = got + jnp.where(self.second, 0.0, mine)
         self.give(j, self.c).start()
 
+    def some(self, low, high, cond):
+        @pl.when(cond)
+        def _():
+            for j in range(low, high):
+                self.step(j)
+
     def steps(self):
-        for j in range(CH):
+        for j in range(self.n):
             self.step(j)
 
     def finish(self):
-        for j in range(CH):
+        for j in range(self.n):
             self.pair(j).wait_send()
             self.give(j, self.c).wait_send()
             self.give(j, 1 - self.c).wait_recv()
@@ -333,17 +347,23 @@
                 self.fwd(j).wait_send()
 
 
-def wgrad(upt, ab, g, r, first):
+DOTS = 3 * AW // 256
+PARTS = 4
+PART = DOTS // PARTS
+TILES = 32
+
+
+def wgrad(upt, ab, g, d, first):
     chips = g.shape[0]
-    for j in range(AW // 256):
-        rhs = [
-            ab[k, pl.ds(r, H), :, 256 * j : 256 * j + 256].reshape(H * W, 256) for k in range(T)
-        ]
-        out = jnp.dot(upt[...], jnp.concatenate(rhs, axis=0), preferred_element_type=F32)
-        for half in range(2):
-            place = pl.ds(5 * (r * 8 + j * 2 + half), 5)
-            part = out[:, 128 * half : 128 * half + 128].reshape(chips, 2, 5, 8, 128)
-            g[:, :, place] = part if first else g[:, :, place] + part
+    r, j = lax.div(d, 4), lax.rem(d, 4)
+    lanes = pl.ds(pl.multiple_of(256 * j, 256), 256)
+    rhs = [ab[k, pl.ds(r, H), :, lanes].reshape(H * W, 256) for k in range(T)]
+    out = jnp.dot(upt[...], jnp.concatenate(rhs, axis=0), preferred_element_type=F32)
+    h, base = lax.div(d, PART), 10 * lax.rem(d, PART)
+    for half in range(2):
+        place = pl.ds(base + 5 * half, 5)
+        part = out[:, 128 * half : 128 * half + 128].reshape(chips, 2, 5, 8, 128)
+        g[:, :, h, place] = part if first else g[:, :, h, place] + part
 
 
 def loop_where(count, cond, step):
@@ -358,14 +378,15 @@
 
 
 def k_all(dims, *refs):
-    (index, cstate, cdrift, cnoise, lat, rg, noise, weight, table, gain) = refs[:10]
-    traj, out = refs[10:12]
-    (p, sp, run, run2, dact, ab1, ab2, abu, wr, wd, mod, st, st2, upt1, upt2) = refs[12:27]
-    hal1, hal2 = refs[27:33], refs[33:39]
-    gat1, gat2, gat3 = refs[39:42], refs[42:45], refs[45:48]
-    ch1, ch2, ch3 = refs[48:55], refs[55:62], refs[62:69]
-    g, ra, s, ry, rz, s1, rz1, ry1, s2, rx = refs[69:79]
-    sems = refs[79:]
+    (index, cstate, cdrift, cnoise, lat, rg, noise_h, weight_h, table_h, gain) = refs[:10]
+    run_h, off_h, out = refs[10:13]
+    (p, sp, run, run2, dact, ab1, ab2, abu, wr, wd, mod, st, st2, upt1, upt2) = refs[13:28]
+    hal1, hal2 = refs[28:34], refs[34:40]
+    gat1, gat2, gat3 = refs[40:43], refs[43:46], refs[46:49]
+    ch1, ch2, ch3 = refs[49:56], refs[56:63], refs[63:70]
+    g, ra, s, ry, rz, s1, rz1, ry1, s2, rx, fin = refs[70:81]
+    noise, weight, table, local = refs[81:85]
+    sems = refs[85:]
     sa, sb, sc_, sd, se = sems[0::2]
     qa, qb, qc, qd, qe = sems[1::2]
     w = Where(dims)
@@ -380,6 +401,12 @@
         return q, w.dev(2 * q + c, w.y, w.x)
 
     devs = w.tiles() + [partner] + [chip(d)[1] for d in range(1, chips)]
+    loads = [
+        pltpu.make_async_copy(a, b, local.at[i])
+        for i, (a, b) in enumerate(((weight_h, weight), (table_h, table), (noise_h, noise)))
+    ]
+    for cp in loads:
+        cp.start()
     greet(devs)
 
     def fill(i, _):
@@ -399,29 +426,38 @@
     for cp in copies1:
         cp.start()
 
-    pack_weights(weight, wr, wd)
-    for k in range(T):
-        mod[k : k + 1, :] = gain[...] * (1.0 + table[pl.ds(index[k], 1), :])
-    turned = rg[...].reshape(H * W, C).T
-    for k in range(T):
-        upt2[:, k * H * W : (k + 1) * H * W] = (cdrift[k] * turned).astype(BF16)
-    g[:, :, 120:128] = jnp.zeros((chips, 2, 8, 8, 128), F32)
-    for cp in copies1:
+    for cp in loads:
         cp.wait()
-    halo_unpack(p, 2, hal1[1], hal1[3])
-
-    def up_row(i, _):
-        mask = edge_mask(w, i)
-        v = jnp.where(mask, p[1, i], 0.0)
-        for k in range(T):
-            pack_row(abu, k, i, cdrift[k] * v)
-        return 0
-
-    lax.fori_loop(0, HP, up_row, 0)
+    pack_forward(weight, wr)
+    step = lax.broadcasted_iota(jnp.int32, (1, table.shape[1]), 1)
+    hot = jnp.concatenate([(step == index[k]).astype(F32) for k in range(T)] * 2, axis=0)
+    rows = lax.dot_general(
+        hot, table[...], (((1,), (1,)), ((), ())), precision=HI, preferred_element_type=F32
+    )
+    mod[...] = gain[...].reshape(1, C) * (1.0 + rows[0:T])
     gather_wait(w, *gat1, sent1)
     center, inv = moments(gat1[0], w)
     st[0:T] = center
     st[T:] = inv
+    for cp in copies1:
+        cp.wait()
+    halo_unpack(p, 2, hal1[1], hal1[3])
+
+    def prepare():
+        pack_backward(weight, wd)
+        turned = rg[...].reshape(H * W, C).T
+        for k in range(T):
+            upt2[:, k * H * W : (k + 1) * H * W] = (cdrift[k] * turned).astype(BF16)
+        for h in range(PARTS):
+            g[:, :, h, 10 * PART : TILES] = jnp.zeros((chips, 2, TILES - 10 * PART, 8, 128), F32)
+
+        def up_row(i, _):
+            v = jnp.where(edge_mask(w, i), p[1, i], 0.0)
+            for k in range(T):
+                pack_row(abu, k, i, cdrift[k] * v)
+            return 0
+
+        lax.fori_loop(0, HP, up_row, 0)
 
     def act1(k, _):
         build_act(w, p, 0, st, mod, ab1, k)
@@ -444,15 +480,20 @@
 
     for j in range(CH):
         sweep(lambda k, j: lat[pl.ds(ROWS * j, ROWS)], ab1, run, j)
-        chain1.pair(j).start()
+        chain1.pair(2 * j).start()
+        chain1.pair(2 * j + 1).start()
+        if j > 0:
+            chain1.some(2 * j - 2, 2 * j, chain1.x == 0)
 
     def back(j, _):
         dact[:, pl.ds(ROWS * j, ROWS)] = conv_rows(abu, j, wd)
         return 0
 
-    early = jnp.clip(2 * (xme - 1), 0, CH)
+    early = jnp.where(xme >= chips - 1, CH, jnp.where(xme == chips - 2, 1, 0))
+    pl.when(xme >= chips - 2)(prepare)
     loop_where(CH, lambda j: j < early, back)
-    chain1.steps()
+    chain1.some(0, 2 * CH - 2, chain1.x > 0)
+    chain1.some(2 * CH - 2, 2 * CH, chain1.x >= 0)
     chain1.finish()
 
     def states(i, _):
@@ -471,6 +512,7 @@
     means, vars_ = tile_moments(lambda f, i: sp[f, i + 1, 0:W, :], T)
     gat2[0][w.me] = jnp.concatenate(means + vars_, axis=0)
     sent2 = gather_start(w, *gat2)
+    pl.when(xme < chips - 2)(prepare)
     loop_where(CH, lambda j: j >= early, back)
     gather_wait(w, *gat2, sent2)
     center, inv = moments(gat2[0], w)
@@ -485,7 +527,7 @@
             plain, cross = acc
             norm = (sp[k, i + 1, 0:W, :] - center) * inv
             pre = norm * m
-            sig = 1.0 / (1.0 + jnp.exp(-pre))
+            sig = 0.5 + 0.5 * jnp.tanh(0.5 * pre)
             d = dact[k, i] * sig * (1.0 + pre * (1.0 - sig)) * m
             dact[k, i] = d
             return plain + d, cross + d * norm
@@ -526,130 +568,182 @@
 
     for j in range(CH):
         lax.fori_loop(0, ROWS, lambda i, z, j=j: through(ROWS * j + i, z), 0)
-        chain2.pair(j).start()
+        chain2.pair(2 * j).start()
+        chain2.pair(2 * j + 1).start()
 
     def second(j, _):
         sweep(lambda k, j: sp[k, pl.ds(1 + ROWS * j, ROWS), 0:W, :], ab2, run2, j)
         return 0
 
-    def weight2(r, _):
-        wgrad(upt2, ab2, g, r, True)
+    def weight2(d, _):
+        wgrad(upt2, ab2, g, d, True)
         return 0
 
     n = jnp.clip(2 * chain2.x, 0, CH)
-    m = jnp.where(chain2.x == chips - 1, 3, 0)
+    m = jnp.where(chain2.x == chips - 1, DOTS, 0)
     loop_where(CH, lambda j: j < n, second)
-    loop_where(3, lambda r: r < m, weight2)
+    loop_where(DOTS, lambda d: d < m, weight2)
     chain2.steps()
     loop_where(CH, lambda j: j >= n, second)
     for j in range(CH):
         chain3.pair(j).start()
-    loop_where(3, lambda r: r >= m, weight2)
+    store = pltpu.make_async_copy(run2, run_h, local.at[3])
+    store.start()
+    loop_where(DOTS, lambda d: d >= m, weight2)
     chain2.finish()
+    chain3.some(0, CH, chain3.x == 0)
 
     for k in range(T):
         adj = chain2.off[...] + run[k + 1] if k + 1 < T else chain2.off[...]
         up = (cdrift[k] * adj).reshape(H * W, C).astype(BF16)
         upt1[:, k * H * W : (k + 1) * H * W] = up.T
 
-    def pairs(r):
-        place = pl.ds(40 * r, 40)
-        return rcopy(g.at[:, 1 - c, place], ra.at[:, place], sa.at[r], qa.at[r], partner)
-
-    for r in range(3):
-        wgrad(upt1, ab1, g, r, False)
-        pairs(r).start()
+    def pairs(h):
+        return rcopy(g.at[:, 1 - c, h], ra.at[h], sa.at[h], qa.at[h], partner)
+
     done = []
 
     def go(cp):
         cp.start()
         done.append(cp)
 
-    per = g.shape[2] // w.nd
-
-    def add(q, _):
-        place = pl.ds(per * q, per)
+    def weight1(d, _):
+        wgrad(upt1, ab1, g, d, False)
+        return 0
+
+    per = s.shape[4]
+    two = per // 2
+
+    def add(h):
+        pairs(h).wait_recv()
+
+        def one(q, _):
+            place = pl.ds(per * q, per)
+            for x in range(chips):
+                s[h, x, lax.div(q, nx), lax.rem(q, nx)] = g[x, c, h, place] + ra[h, x, place]
+            return 0
+
+        lax.fori_loop(0, w.nd, one, 0)
+
+    def along(h):
+        b = h * (nx + ny)
+        for d in range(1, nx):
+            q = lax.rem(w.x + d, nx)
+            go(rcopy(s.at[h, :, :, q, 0:two], rz.at[h, w.x], sb.at[b + d], qb.at[b + w.x], w.shift(0, d)))
+        for d in range(1, ny):
+            q = lax.rem(w.y + d, ny)
+            b2 = b + nx
+            go(rcopy(s.at[h, :, q, :, two:per], ry.at[h, w.y], sb.at[b2 + d], qb.at[b2 + w.y], w.shift(d, 0)))
+
+    def across(h):
+        b = h * (nx + ny)
+        for d in range(1, nx):
+            q = lax.rem(w.x + d, nx)
+            rcopy(rz.at[h, q], rz.at[h, q], sb.at[b + d], qb.at[b + q], partner).wait_recv()
+        for d in range(1, ny):
+            q = lax.rem(w.y + d, ny)
+            b2 = b + nx
+            rcopy(ry.at[h, q], ry.at[h, q], sb.at[b2 + d], qb.at[b2 + q], partner).wait_recv()
+
+        def join(x, _):
+            for i in range(ny):
+                acc = s[h, x, i, w.x, 0:two]
+                for d in range(1, nx):
+                    acc += rz[h, lax.rem(w.x + d, nx), x, i]
+                s1[h, 0, x, i] = acc
+            for j in range(nx):
+                acc = s[h, x, w.y, j, two:per]
+                for d in range(1, ny):
+                    acc += ry[h, lax.rem(w.y + d, ny), x, j]
+                s1[h, 1, x, j] = acc
+            return 0
+
+        lax.fori_loop(0, chips, join, 0)
+        b = h * (nx + ny)
+        for d in range(1, ny):
+            q = lax.rem(w.y + d, ny)
+            go(rcopy(s1.at[h, 0, :, q], rz1.at[h, w.y], sc_.at[b + d], qc.at[b + w.y], w.shift(d, 0)))
+        for d in range(1, nx):
+            q = lax.rem(w.x + d, nx)
+            b2 = b + ny
+            go(rcopy(s1.at[h, 1, :, q], ry1.at[h, w.x], sc_.at[b2 + d], qc.at[b2 + w.x], w.shift(0, d)))
+
+    def chips_out(h):
+        b = h * (nx + ny)
+        for d in range(1, ny):
+            q = lax.rem(w.y + d, ny)
+            rcopy(rz1.at[h, q], rz1.at[h, q], sc_.at[b + d], qc.at[b + q], partner).wait_recv()
+        for d in range(1, nx):
+            q = lax.rem(w.x + d, nx)
+            b2 = b + ny
+            rcopy(ry1.at[h, q], ry1.at[h, q], sc_.at[b2 + d], qc.at[b2 + q], partner).wait_recv()
         for x in range(chips):
-            s[x, lax.div(q, nx), lax.rem(q, nx)] = g[x, c, place] + ra[x, place]
-        return 0
-
+            acc = s1[h, 0, x, w.y]
+            for d in range(1, ny):
+                acc += rz1[h, lax.rem(w.y + d, ny), x]
+            s2[h, x, 0:two] = acc
+            acc = s1[h, 1, x, w.x]
+            for d in range(1, nx):
+                acc += ry1[h, lax.rem(w.x + d, nx), x]
+            s2[h, x, two:per] = acc
+        for d in range(1, chips):
+            q, dev = chip(d)
+            go(rcopy(s2.at[h, q], rx.at[h, xme], sd.at[h * chips + d], qd.at[h * chips + xme], dev))
+
+    def spread(h):
+        for d in range(1, chips):
+            q, dev = chip(d)
+            rcopy(rx.at[h, q], rx.at[h, q], sd.at[h * chips + d], qd.at[h * chips + q], dev).wait_recv()
+        acc = s2[h, xme]
+        for d in range(1, chips):
+            acc += rx[h, lax.rem(xme + d, chips)]
+        fin[h, w.me] = acc
+        b = pl.ds(h * w.nd, w.nd)
+        return gather_start(w, fin.at[h], se.at[b], qe.at[b])
+
+    for h in range(PARTS):
+        lax.fori_loop(PART * h, PART * h + PART, weight1, 0)
+        pairs(h).start()
+        if h > 1:
+            add(h - 2)
+            along(h - 2)
+    for h in (PARTS - 2, PARTS - 1):
+        add(h)
+        along(h)
+    chain3.some(0, CH, chain3.x == 1)
+    across(0)
+    across(1)
+    chain3.some(0, CH, chain3.x == 2)
+    across(2)
+    chips_out(0)
+    chips_out(1)
+    across(3)
+    sent = [spread(0), spread(1)]
+    chips_out(2)
+    chain3.some(0, CH, chain3.x == chips - 1)
+    chips_out(3)
+    sent += [spread(2), spread(3)]
+    chain3.finish()
+    store2 = pltpu.make_async_copy(chain3.off, off_h, local.at[4])
+    store2.start()
+    for h in range(PARTS):
+        b = pl.ds(h * w.nd, w.nd)
+        gather_wait(w, fin.at[h], se.at[b], qe.at[b], sent[h])
     for r in range(3):
-        pairs(r).wait_recv()
-        lax.fori_loop(5 * r, 5 * r + 5, add, 0)
-    for x in range(chips):
-        s[x, ny - 1, nx - 1] = jnp.zeros((per, 8, 128), F32)
-    for d in range(1, nx):
-        q = lax.rem(w.x + d, nx)
-        go(rcopy(s.at[:, :, q, 0:4], rz.at[w.x], sb.at[d], qb.at[w.x], w.shift(0, d)))
-    for d in range(1, ny):
-        q = lax.rem(w.y + d, ny)
-        go(rcopy(s.at[:, q, :, 4:8], ry.at[w.y], sb.at[nx + d], qb.at[nx + w.y], w.shift(d, 0)))
-    chain3.steps()
-    for d in range(1, nx):
-        q = lax.rem(w.x + d, nx)
-        rcopy(rz.at[q], rz.at[q], sb.at[d], qb.at[q], partner).wait_recv()
-    for d in range(1, ny):
-        q = lax.rem(w.y + d, ny)
-        rcopy(ry.at[q], ry.at[q], sb.at[nx + d], qb.at[nx + q], partner).wait_recv()
-
-    def join(x, _):
-        for i in range(ny):
-            acc = s[x, i, w.x, 0:4]
-            for d in range(1, nx):
-                acc += rz[lax.rem(w.x + d, nx), x, i]
-            s1[0, x, i] = acc
-        for j in range(nx):
-            acc = s[x, w.y, j, 4:8]
-            for d in range(1, ny):
-                acc += ry[lax.rem(w.y + d, ny), x, j]
-            s1[1, x, j] = acc
-        return 0
-
-    lax.fori_loop(0, chips, join, 0)
-    for d in range(1, ny):
-        q = lax.rem(w.y + d, ny)
-        go(rcopy(s1.at[0, :, q], rz1.at[w.y], sc_.at[d], qc.at[w.y], w.shift(d, 0)))
-    for d in range(1, nx):
-        q = lax.rem(w.x + d, nx)
-        go(rcopy(s1.at[1, :, q], ry1.at[w.x], sc_.at[ny + d], qc.at[ny + w.x], w.shift(0, d)))
-    chain3.finish()
-
-    def final(i, _):
-        o2, base = chain3.off[i], lat[i]
-        for k in range(T):
-            traj[k, i] = base + (o2 + run2[k, i])
-        return 0
-
-    lax.fori_loop(0, H, final, 0)
-    for d in range(1, ny):
-        q = lax.rem(w.y + d, ny)
-        rcopy(rz1.at[q], rz1.at[q], sc_.at[d], qc.at[q], partner).wait_recv()
-    for d in range(1, nx):
-        q = lax.rem(w.x + d, nx)
-        rcopy(ry1.at[q], ry1.at[q], sc_.at[ny + d], qc.at[ny + q], partner).wait_recv()
-    for x in range(chips):
-        acc = s1[0, x, w.y]
-        for d in range(1, ny):
-            acc += rz1[lax.rem(w.y + d, ny), x]
-        s2[x, 0:4] = acc
-        acc = s1[1, x, w.x]
-        for d in range(1, nx):
-            acc += ry1[lax.rem(w.x + d, nx), x]
-        s2[x, 4:8] = acc
-    for d in range(1, chips):
-        q, dev = chip(d)
-        go(rcopy(s2.at[q], rx.at[xme], sd.at[d], qd.at[xme], dev))
-    for d in range(1, chips):
-        q, dev = chip(d)
-        rcopy(rx.at[q], rx.at[q], sd.at[d], qd.at[q], dev).wait_recv()
-    acc = s2[xme]
-    for d in range(1, chips):
-        acc += rx[lax.rem(xme + d, chips)]
-    out[w.me] = acc
-    sent = gather_start(w, out, se, qe)
-    gather_wait(w, out, se, qe, sent)
-    for r in range(3):
-        pairs(r).wait_send()
+        cols = []
+        for l in range(8):
+            d = 4 * r + l // 2
+            first_tile = 10 * (d % PART) + 5 * (l % 2)
+            tiles = [fin[d // PART, t // per, t % per] for t in range(first_tile, first_tile + 5)]
+            cols.append(jnp.concatenate(tiles, axis=0))
+        whole = jnp.concatenate(cols, axis=1)
+        for q in range(3):
+            out[r, q, :, 0:256] = whole[:, 256 * q : 256 * q + 256]
+            out[r, q, :, 256:C] = whole[:, 768 + 64 * q : 832 + 64 * q]
+    store.wait()
+    store2.wait()
+    for h in range(PARTS):
+        pairs(h).wait_send()
     for cp in done:
         cp.wait_send()
 
@@ -658,7 +752,7 @@
     nt, ny, nx = dims
     nd = ny * nx
     chips = nt // 2
-    per = 128 // nd
+    per = TILES // nd
     half = per // 2
     dma = pltpu.SemaphoreType.DMA
     vmem = pltpu.VMEM
@@ -682,41 +776,43 @@
         vmem((C, T * H * W), BF16),
     ]
     scratch += halo_scratch(2) + halo_scratch(T)
-    scratch += gather_scratch(nd) * 3 + chain_scratch() * 3
+    scratch += gather_scratch(nd) * 3 + chain_scratch(2 * CH) * 2 + chain_scratch(CH)
     scratch += [
-        vmem((chips, 2, 128, 8, 128), F32),
-        vmem((chips, 128, 8, 128), F32),
-        vmem((chips, ny, nx, per, 8, 128), F32),
-        vmem((ny, chips, nx, half, 8, 128), F32),
-        vmem((nx, chips, ny, half, 8, 128), F32),
-        vmem((2, chips, max(nx, ny), half, 8, 128), F32),
-        vmem((ny, chips, half, 8, 128), F32),
-        vmem((nx, chips, half, 8, 128), F32),
-        vmem((chips, per, 8, 128), F32),
-        vmem((chips, per, 8, 128), F32),
+        vmem((chips, 2, PARTS, TILES, 8, 128), F32),
+        vmem((PARTS, chips, TILES, 8, 128), F32),
+        vmem((PARTS, chips, ny, nx, per, 8, 128), F32),
+        vmem((PARTS, ny, chips, nx, half, 8, 128), F32),
+        vmem((PARTS, nx, chips, ny, half, 8, 128), F32),
+        vmem((PARTS, 2, chips, max(nx, ny), half, 8, 128), F32),
+        vmem((PARTS, ny, chips, half, 8, 128), F32),
+        vmem((PARTS, nx, chips, half, 8, 128), F32),
+        vmem((PARTS, chips, per, 8, 128), F32),
+        vmem((PARTS, chips, per, 8, 128), F32),
+        vmem((PARTS, nd, per, 8, 128), F32),
+        vmem(noise.shape, BF16),
+        vmem(weight.shape, BF16),
+        vmem(table.shape[::-1], F32),
+        dma((5,)),
     ]
-    for count in (3, nx + ny, nx + ny, chips, nd):
-        scratch += [dma((count,)), dma((count,))]
-    traj, out = pl.pallas_call(
+    for count in (1, nx + ny, nx + ny, chips, nd):
+        scratch += [dma((PARTS * count,)), dma((PARTS * count,))]
+    run, off, out = pl.pallas_call(
         functools.partial(k_all, dims),
         out_shape=(
             jax.ShapeDtypeStruct(field, F32),
-            jax.ShapeDtypeStruct((nd, per, 8, 128), F32),
+            jax.ShapeDtypeStruct((H, W, C), F32),
+            jax.ShapeDtypeStruct((3, 3, C // nt, C), F32),
         ),
-        in_specs=[SM] * 4 + [VM] * 6,
-        out_specs=(VM, VM),
+        in_specs=[SM] * 4 + [VM] * 2 + [ANY] * 3 + [VM],
+        out_specs=(ANY, ANY, VM),
         scratch_shapes=scratch,
         compiler_params=pltpu.CompilerParams(
             vmem_limit_bytes=VLIM, collective_id=0, has_side_effects=True
         ),
         name="picard",
-    )(step_index, coef_state, coef_drift, coef_noise, latent, rg, noise, weight, table, gain[None])
-    tiles = out.reshape(128, 8, 128)[:120].reshape(3, 8, 40, 128)
-    flat = jnp.transpose(tiles, (0, 2, 1, 3)).reshape(3, 40, AW)
-    main = flat[:, :, 0:768].reshape(3, 40, 3, 256)
-    tail = flat[:, :, 768:960].reshape(3, 40, 3, 64)
-    grad = jnp.transpose(jnp.concatenate([main, tail], axis=3), (0, 2, 3, 1))
-    return traj, grad
+    )(step_index, coef_state, coef_drift, coef_noise, latent, rg, noise, weight, table.T, gain)
+    traj = latent[None] + (off[None] + run)
+    return traj, jnp.transpose(out, (0, 1, 3, 2))
 
 
 def solution(mesh):

time: 129 us -> 116 us (0.90)
  Pallas kernels: 119 us -> 111 us
  local copies, waits for them, and re-layouts: 8.45 us -> 0.81 us
  other arithmetic: 0.18 us -> 3.44 us
    pallas_call x1, Pallas kernels: 119 us -> 111 us  [shards(): pl.pallas_call(functools.partial(k_all, dims), out_shape=(jax.ShapeDtypeS...]
    unnamed x5, local copies, waits for them, and re-layouts: 5.62 us -> 0.81 us
    add x0 -> x1, other arithmetic: none -> 3.44 us  [shards(): traj = latent[None] + (off[None] + run)]
where the time goes in v3:
time: 116 us
  Pallas kernels  111 us (96%)
  other arithmetic  3.44 us (3%)
    pallas_call x1, Pallas kernels, shards(): pl.pallas_call(functools.partial(k_all, dims), out_shape=(jax.ShapeDtypeS...  111 us
    add x1, other arithmetic, shards(): traj = latent[None] + (off[None] + run)  3.44 us

profile of v3, /device:TPU:0, one launch (start us, length us, event | category | flops | bytes accessed | tf_op | source)
XLA Modules:
  0.0 115.6 jit_solution(4043713615866527221)
XLA Ops:
  0.6 0.0 copy-start
  0.6 110.6 %picard.1 = (f32[4,16,24,320]{3,2,1,0:T(8,128)}, f32[16,24,320]{2,1,0:T(8,128)}, f32[3,3,40,320]{3,2,1,0:T(8,128)}) custom-call(s32[4]{0:T(128)} %refs_0_.1, f32[4]{0:T(128)} %refs_1_.1, f32[4]{0:T(128)} %refs_2_.1, f32[4]{0:T(128)} %refs_3_.1, f32[16,24,320]{2,1,0:T(8,128)} %refs_4_.1, f32[16,24,320]{2,1,0:T(8,128)} %refs_5_.1, ...), custom_call_target="tpu_custom_call" | custom-call | tf_op jit(solution)/shard_map/picard/pallas_call | solution.py:799
  111.3 0.0 copy-done
  111.3 0.0 copy-start.1
  111.3 3.4 %add_add_fusion = f32[4,16,24,320]{3,2,1,0:T(8,128)} fusion(f32[4,16,24,320]{3,2,1,0:T(8,128)} %get-tuple-element.6, f32[16,24,320]{2,1,0:T(8,128)} %get-tuple-element.5, f32[16,24,320]{2,1,0:T(8,128)S(1)} %copy-done), kind=kLoop, calls=%fused_computation | loop fusion | flops 983040 | bytes 4915200 | tf_op jit(solution)/shard_map/add | solution.py:814
  114.7 0.0 copy-done.1
  114.8 0.8 copy.13
Async XLA Ops:
  0.6 110.7 %copy-start = (f32[16,24,320]{2,1,0:T(8,128)S(1)}, f32[16,24,320]{2,1,0:T(8,128)}, u32[]{:S(2)}) copy-start(f32[16,24,320]{2,1,0:T(8,128)} %refs_4_.1) | copy-start | bytes 1474564
  111.3 3.4 %copy-start.1 = (f32[3,3,40,320]{3,2,1,0:T(8,128)S(1)}, f32[3,3,40,320]{3,2,1,0:T(8,128)}, u32[]{:S(2)}) copy-start(f32[3,3,40,320]{3,2,1,0:T(8,128)} %get-tuple-element.7) | copy-start | bytes 1382404

commit v4 on v3

--- a/solution.py
+++ b/solution.py
@@ -378,17 +378,17 @@
 
 
 def k_all(dims, *refs):
-    (index, cstate, cdrift, cnoise, lat, rg, noise_h, weight_h, table_h, gain) = refs[:10]
+    (index, cstate, cdrift, cnoise, lat_h, rg_h, noise_h, weight_h, table_h, gain) = refs[:10]
     run_h, off_h, out = refs[10:13]
     (p, sp, run, run2, dact, ab1, ab2, abu, wr, wd, mod, st, st2, upt1, upt2) = refs[13:28]
     hal1, hal2 = refs[28:34], refs[34:40]
     gat1, gat2, gat3 = refs[40:43], refs[43:46], refs[46:49]
     ch1, ch2, ch3 = refs[49:56], refs[56:63], refs[63:70]
     g, ra, s, ry, rz, s1, rz1, ry1, s2, rx, fin = refs[70:81]
-    noise, weight, table, local = refs[81:85]
-    sems = refs[85:]
-    sa, sb, sc_, sd, se = sems[0::2]
-    qa, qb, qc, qd, qe = sems[1::2]
+    noise, weight, table, lat, rg, sx, rf, local = refs[81:89]
+    sems = refs[89:]
+    sa, sb, sc_, sd, se, sf = sems[0::2]
+    qa, qb, qc, qd, qe, qf = sems[1::2]
     w = Where(dims)
     chips = w.nt // 2
     c = lax.rem(w.tm, 2)
@@ -403,11 +403,13 @@
     devs = w.tiles() + [partner] + [chip(d)[1] for d in range(1, chips)]
     loads = [
         pltpu.make_async_copy(a, b, local.at[i])
-        for i, (a, b) in enumerate(((weight_h, weight), (table_h, table), (noise_h, noise)))
+        for i, (a, b) in enumerate(((lat_h, lat), (rg_h, rg), (weight_h, weight), (table_h, table), (noise_h, noise)))
     ]
     for cp in loads:
         cp.start()
     greet(devs)
+    for cp in loads[:2]:
+        cp.wait()
 
     def fill(i, _):
         for f, ref in ((0, lat), (1, rg)):
@@ -426,7 +428,7 @@
     for cp in copies1:
         cp.start()
 
-    for cp in loads:
+    for cp in loads[2:]:
         cp.wait()
     pack_forward(weight, wr)
     step = lax.broadcasted_iota(jnp.int32, (1, table.shape[1]), 1)
@@ -459,11 +461,20 @@
 
         lax.fori_loop(0, HP, up_row, 0)
 
-    def act1(k, _):
-        build_act(w, p, 0, st, mod, ab1, k)
-        return 0
-
-    lax.fori_loop(0, T, act1, 0)
+    def act_row(i):
+        center, inv = st[0:1, :], st[T : T + 1, :]
+        norm = (p[0, i] - center) * inv
+        mask = edge_mask(w, i)
+        for k in range(T):
+            pre = norm * mod[k : k + 1, :]
+            act = pre * (0.5 + 0.5 * jnp.tanh(0.5 * pre))
+            pack_row(ab1, k, i, jnp.where(mask, act, 0.0))
+
+    def act1(i, _):
+        act_row(i)
+        return 0
+
+    lax.fori_loop(0, ROWS + 2, act1, 0)
     chain1 = Chain(w, run.at[T - 1], ch1, False)
     chain3 = Chain(w, run2.at[T - 1], ch3, False)
 
@@ -479,6 +490,9 @@
             dst[k, rows] = acc
 
     for j in range(CH):
+        if j + 1 < CH:
+            for i in range(ROWS):
+                act_row(ROWS * (j + 1) + 2 + i)
         sweep(lambda k, j: lat[pl.ds(ROWS * j, ROWS)], ab1, run, j)
         chain1.pair(2 * j).start()
         chain1.pair(2 * j + 1).start()
@@ -587,7 +601,7 @@
     loop_where(CH, lambda j: j >= n, second)
     for j in range(CH):
         chain3.pair(j).start()
-    store = pltpu.make_async_copy(run2, run_h, local.at[3])
+    store = pltpu.make_async_copy(run2, run_h, local.at[5])
     store.start()
     loop_where(DOTS, lambda d: d >= m, weight2)
     chain2.finish()
@@ -625,59 +639,84 @@
 
         lax.fori_loop(0, w.nd, one, 0)
 
+    def chips_first():
+        for d in range(1, chips):
+            q, dev = chip(d)
+            go(rcopy(s.at[0, q], rf.at[xme], sf.at[d], qf.at[xme], dev))
+
+    def chips_join():
+        for d in range(1, chips):
+            q, dev = chip(d)
+            rcopy(rf.at[q], rf.at[q], sf.at[d], qf.at[q], dev).wait_recv()
+
+        def one(i, _):
+            acc = s[0, xme, i]
+            for d in range(1, chips):
+                acc += rf[lax.rem(xme + d, chips), i]
+            sx[0, i] = acc
+            return 0
+
+        lax.fori_loop(0, ny, one, 0)
+
+    def source(h):
+        return (s.at[h], chips) if h else (sx, 1)
+
     def along(h):
         b = h * (nx + ny)
+        src, n = source(h)
         for d in range(1, nx):
             q = lax.rem(w.x + d, nx)
-            go(rcopy(s.at[h, :, :, q, 0:two], rz.at[h, w.x], sb.at[b + d], qb.at[b + w.x], w.shift(0, d)))
+            go(rcopy(src.at[:, :, q, 0:two], rz.at[h, w.x, 0:n], sb.at[b + d], qb.at[b + w.x], w.shift(0, d)))
         for d in range(1, ny):
             q = lax.rem(w.y + d, ny)
             b2 = b + nx
-            go(rcopy(s.at[h, :, q, :, two:per], ry.at[h, w.y], sb.at[b2 + d], qb.at[b2 + w.y], w.shift(d, 0)))
+            go(rcopy(src.at[:, q, :, two:per], ry.at[h, w.y, 0:n], sb.at[b2 + d], qb.at[b2 + w.y], w.shift(d, 0)))
 
     def across(h):
         b = h * (nx + ny)
+        src, n = source(h)
         for d in range(1, nx):
             q = lax.rem(w.x + d, nx)
-            rcopy(rz.at[h, q], rz.at[h, q], sb.at[b + d], qb.at[b + q], partner).wait_recv()
+            rcopy(rz.at[h, q, 0:n], rz.at[h, q, 0:n], sb.at[b + d], qb.at[b + q], partner).wait_recv()
         for d in range(1, ny):
             q = lax.rem(w.y + d, ny)
             b2 = b + nx
-            rcopy(ry.at[h, q], ry.at[h, q], sb.at[b2 + d], qb.at[b2 + q], partner).wait_recv()
+            rcopy(ry.at[h, q, 0:n], ry.at[h, q, 0:n], sb.at[b2 + d], qb.at[b2 + q], partner).wait_recv()
 
         def join(x, _):
             for i in range(ny):
-                acc = s[h, x, i, w.x, 0:two]
+                acc = src[x, i, w.x, 0:two]
                 for d in range(1, nx):
                     acc += rz[h, lax.rem(w.x + d, nx), x, i]
                 s1[h, 0, x, i] = acc
             for j in range(nx):
-                acc = s[h, x, w.y, j, two:per]
+                acc = src[x, w.y, j, two:per]
                 for d in range(1, ny):
                     acc += ry[h, lax.rem(w.y + d, ny), x, j]
                 s1[h, 1, x, j] = acc
             return 0
 
-        lax.fori_loop(0, chips, join, 0)
+        lax.fori_loop(0, n, join, 0)
         b = h * (nx + ny)
         for d in range(1, ny):
             q = lax.rem(w.y + d, ny)
-            go(rcopy(s1.at[h, 0, :, q], rz1.at[h, w.y], sc_.at[b + d], qc.at[b + w.y], w.shift(d, 0)))
+            go(rcopy(s1.at[h, 0, 0:n, q], rz1.at[h, w.y, 0:n], sc_.at[b + d], qc.at[b + w.y], w.shift(d, 0)))
         for d in range(1, nx):
             q = lax.rem(w.x + d, nx)
             b2 = b + ny
-            go(rcopy(s1.at[h, 1, :, q], ry1.at[h, w.x], sc_.at[b2 + d], qc.at[b2 + w.x], w.shift(0, d)))
+            go(rcopy(s1.at[h, 1, 0:n, q], ry1.at[h, w.x, 0:n], sc_.at[b2 + d], qc.at[b2 + w.x], w.shift(0, d)))
 
     def chips_out(h):
         b = h * (nx + ny)
+        n = source(h)[1]
         for d in range(1, ny):
             q = lax.rem(w.y + d, ny)
-            rcopy(rz1.at[h, q], rz1.at[h, q], sc_.at[b + d], qc.at[b + q], partner).wait_recv()
+            rcopy(rz1.at[h, q, 0:n], rz1.at[h, q, 0:n], sc_.at[b + d], qc.at[b + q], partner).wait_recv()
         for d in range(1, nx):
             q = lax.rem(w.x + d, nx)
             b2 = b + ny
-            rcopy(ry1.at[h, q], ry1.at[h, q], sc_.at[b2 + d], qc.at[b2 + q], partner).wait_recv()
-        for x in range(chips):
+            rcopy(ry1.at[h, q, 0:n], ry1.at[h, q, 0:n], sc_.at[b2 + d], qc.at[b2 + q], partner).wait_recv()
+        for x in range(n):
             acc = s1[h, 0, x, w.y]
             for d in range(1, ny):
                 acc += rz1[h, lax.rem(w.y + d, ny), x]
@@ -686,16 +725,16 @@
             for d in range(1, nx):
                 acc += ry1[h, lax.rem(w.x + d, nx), x]
             s2[h, x, two:per] = acc
-        for d in range(1, chips):
+        for d in range(1, chips if h else 1):
             q, dev = chip(d)
             go(rcopy(s2.at[h, q], rx.at[h, xme], sd.at[h * chips + d], qd.at[h * chips + xme], dev))
 
     def spread(h):
-        for d in range(1, chips):
+        for d in range(1, chips if h else 1):
             q, dev = chip(d)
             rcopy(rx.at[h, q], rx.at[h, q], sd.at[h * chips + d], qd.at[h * chips + q], dev).wait_recv()
-        acc = s2[h, xme]
-        for d in range(1, chips):
+        acc = s2[h, xme] if h else s2[0, 0]
+        for d in range(1, chips if h else 1):
             acc += rx[h, lax.rem(xme + d, chips)]
         fin[h, w.me] = acc
         b = pl.ds(h * w.nd, w.nd)
@@ -704,27 +743,33 @@
     for h in range(PARTS):
         lax.fori_loop(PART * h, PART * h + PART, weight1, 0)
         pairs(h).start()
-        if h > 1:
-            add(h - 2)
-            along(h - 2)
-    for h in (PARTS - 2, PARTS - 1):
+        if h == 2:
+            add(0)
+            chips_first()
+        if h == 3:
+            add(1)
+            along(1)
+    for h in (2, 3):
         add(h)
         along(h)
     chain3.some(0, CH, chain3.x == 1)
-    across(0)
     across(1)
-    chain3.some(0, CH, chain3.x == 2)
+    chips_join()
+    along(0)
     across(2)
-    chips_out(0)
     chips_out(1)
     across(3)
-    sent = [spread(0), spread(1)]
+    chain3.some(0, CH, chain3.x == 2)
+    across(0)
+    sent = [None, spread(1)]
     chips_out(2)
+    chips_out(3)
+    chips_out(0)
+    sent[0] = spread(0)
+    sent += [spread(2), spread(3)]
     chain3.some(0, CH, chain3.x == chips - 1)
-    chips_out(3)
-    sent += [spread(2), spread(3)]
     chain3.finish()
-    store2 = pltpu.make_async_copy(chain3.off, off_h, local.at[4])
+    store2 = pltpu.make_async_copy(chain3.off, off_h, local.at[6])
     store2.start()
     for h in range(PARTS):
         b = pl.ds(h * w.nd, w.nd)
@@ -792,10 +837,15 @@
         vmem(noise.shape, BF16),
         vmem(weight.shape, BF16),
         vmem(table.shape[::-1], F32),
-        dma((5,)),
+        vmem((H, W, C), F32),
+        vmem((H, W, C), F32),
+        vmem((1, ny, nx, per, 8, 128), F32),
+        vmem((chips, ny, nx, per, 8, 128), F32),
+        dma((7,)),
     ]
     for count in (1, nx + ny, nx + ny, chips, nd):
         scratch += [dma((PARTS * count,)), dma((PARTS * count,))]
+    scratch += [dma((chips,)), dma((chips,))]
     run, off, out = pl.pallas_call(
         functools.partial(k_all, dims),
         out_shape=(
@@ -803,7 +853,7 @@
             jax.ShapeDtypeStruct((H, W, C), F32),
             jax.ShapeDtypeStruct((3, 3, C // nt, C), F32),
         ),
-        in_specs=[SM] * 4 + [VM] * 2 + [ANY] * 3 + [VM],
+        in_specs=[SM] * 4 + [ANY] * 5 + [VM],
         out_specs=(ANY, ANY, VM),
         scratch_shapes=scratch,
         compiler_params=pltpu.CompilerParams(

time: 116 us -> 114 us (0.983)
  Pallas kernels: 111 us -> 109 us
    pallas_call x1, Pallas kernels: 111 us -> 109 us  [shards(): pl.pallas_call(functools.partial(k_all, dims), out_shape=(jax.ShapeDtypeS...]
where the time goes in v4:
time: 114 us
  Pallas kernels  109 us (96%)
  other arithmetic  3.44 us (3%)
    pallas_call x1, Pallas kernels, shards(): pl.pallas_call(functools.partial(k_all, dims), out_shape=(jax.ShapeDtypeS...  109 us
    add x1, other arithmetic, shards(): traj = latent[None] + (off[None] + run)  3.44 us

profile of v4, /device:TPU:0, one launch (start us, length us, event | category | flops | bytes accessed | tf_op | source)
XLA Modules:
  0.0 113.8 jit_solution(17255095469261739189)
XLA Ops:
  0.6 0.0 copy-start
  0.6 108.8 %picard.1 = (f32[4,16,24,320]{3,2,1,0:T(8,128)}, f32[16,24,320]{2,1,0:T(8,128)}, f32[3,3,40,320]{3,2,1,0:T(8,128)}) custom-call(s32[4]{0:T(128)} %refs_0_.1, f32[4]{0:T(128)} %refs_1_.1, f32[4]{0:T(128)} %refs_2_.1, f32[4]{0:T(128)} %refs_3_.1, f32[16,24,320]{2,1,0:T(8,128)} %refs_4_.1, f32[16,24,320]{2,1,0:T(8,128)} %refs_5_.1, ...), custom_call_target="tpu_custom_call" | custom-call | tf_op jit(solution)/shard_map/picard/pallas_call | solution.py:849
  109.5 0.0 copy-done
  109.5 0.0 copy-start.1
  109.5 3.4 %add_add_fusion = f32[4,16,24,320]{3,2,1,0:T(8,128)} fusion(f32[4,16,24,320]{3,2,1,0:T(8,128)} %get-tuple-element.6, f32[16,24,320]{2,1,0:T(8,128)} %get-tuple-element.5, f32[16,24,320]{2,1,0:T(8,128)S(1)} %copy-done), kind=kLoop, calls=%fused_computation | loop fusion | flops 983040 | bytes 4915200 | tf_op jit(solution)/shard_map/add | solution.py:864
  113.0 0.0 copy-done.1
  113.0 0.8 copy.13
Async XLA Ops:
  0.6 108.9 %copy-start = (f32[16,24,320]{2,1,0:T(8,128)S(1)}, f32[16,24,320]{2,1,0:T(8,128)}, u32[]{:S(2)}) copy-start(f32[16,24,320]{2,1,0:T(8,128)} %refs_4_.1) | copy-start | bytes 1474564
  109.5 3.4 %copy-start.1 = (f32[3,3,40,320]{3,2,1,0:T(8,128)S(1)}, f32[3,3,40,320]{3,2,1,0:T(8,128)}, u32[]{:S(2)}) copy-start(f32[3,3,40,320]{3,2,1,0:T(8,128)} %get-tuple-element.7) | copy-start | bytes 1382404
